TPU v7x, 32 devices: a whole 2x2x4 slice. The times are simulated.
32 devices in a mesh: clip: 4 (over x, core), frame: 8 (over z, y).
Axes of the slice: x: 2, y: 2, z: 4, core: 2. Of those that a mesh axis runs over, the one named last changes fastest.
Arguments:
- video_tokens: bfloat16 [8, 32, 256, 1024], P('clip', 'frame'), parts along dimension 0, may hold values from -6 to 6
- frame_count: int32 [8], P('clip'), parts along dimension 0, may hold values from 8 to 32, as said below
- token_count: int32 [8], P('clip'), parts along dimension 0, may hold values from 128 to 256, as said below
- time_gain: float32 [1024], replicated, may hold values from 0.5 to 2
- time_qkv: bfloat16 [1024, 1536], replicated
- time_out: bfloat16 [512, 1024], replicated, may hold values from -0.5 to 0.5
- space_gain: float32 [1024], replicated, may hold values from 0.5 to 2
- space_qkv: bfloat16 [1024, 1536], replicated
- space_out: bfloat16 [512, 1024], replicated, may hold values from -0.5 to 0.5
Outputs:
- block_out: bfloat16 [8, 32, 256, 1024], P('clip', 'frame'), parts along dimension 0
There are 4 independent parts, one for each index of `clip`. A program takes and returns all parts, laid end to end along the dimension named above; an argument that names none is the same for every part. Nothing has to cross between parts.
Inputs may be any that keep to these rules, and one draw needn't show every extreme that they name: `frame_count`: frames of each clip; in every draw some clip has all 32. `token_count`: tokens of each frame; in every draw some clip has all 256.
All inputs are finite; a program needn't handle non-finite values.
Results may differ from a plain program's by a relative error of at most 0.025.
The roundings to bfloat16 on the way count: a program that leaves them out, or rounds other values in their place, can miss the bound.
Values may be sent and summed in bfloat16 or wider, within the bound.
No kernel may reach another device: no remote copies, remote signals or barrier semaphores. Data moves between devices by JAX's collectives and lax.ppermute only.
A program may use at most 128 MiB of HBM per device.

v0:
```python
import functools

import jax
import jax.numpy as jnp
from jax import lax
from jax.experimental import pallas as pl
from jax.experimental.pallas import tpu as pltpu
from jax.sharding import PartitionSpec as P

HEADS = 8
HD = 64
HW = 512
ROWS = 16
NEG = -1e30
VMEM_LIMIT = 50 * 1024 * 1024
ANY = pl.BlockSpec(memory_space=pl.ANY)


def normalise(values, gain):
    centre = values - jnp.mean(values, axis=-1, keepdims=True)
    spread = jnp.mean(centre * centre, axis=-1, keepdims=True)
    return (centre * lax.rsqrt(spread + 1e-05) * gain).astype(jnp.bfloat16)


def attend(qkv_ref, rows, bias, out_ref):
    count = rows.size
    low = lax.broadcasted_iota(jnp.int32, (count, 2 * HD), 1) < HD
    zero = jnp.zeros((count, 2 * HD), jnp.bfloat16)
    for pair in range(HEADS // 2):
        cols = pair * 2 * HD
        q = qkv_ref[rows, cols : cols + 2 * HD]
        k = qkv_ref[rows, HW + cols : HW + cols + 2 * HD]
        v = qkv_ref[rows, 2 * HW + cols : 2 * HW + cols + 2 * HD]
        parts = []
        for keys in (jnp.where(low, k, zero), jnp.where(low, zero, k)):
            scores = lax.dot_general(q, keys, (((1,), (1,)), ((), ())), preferred_element_type=jnp.float32)
            scores = scores + bias
            expo = jnp.exp(scores - jnp.max(scores, axis=-1, keepdims=True))
            weights = (expo * (1.0 / jnp.sum(expo, axis=-1, keepdims=True))).astype(jnp.bfloat16)
            parts.append(jnp.dot(weights, v, preferred_element_type=jnp.float32))
        out_ref[rows, cols : cols + 2 * HD] = jnp.where(low, parts[0], parts[1]).astype(jnp.bfloat16)


def project_heads(normed, weight_ref, qkv_ref):
    for part in range(3):
        result = jnp.dot(normed, weight_ref[:, part * HW : (part + 1) * HW], preferred_element_type=jnp.float32)
        if part == 0:
            result = result * HD ** (-0.5)
        qkv_ref[:, part * HW : (part + 1) * HW] = result.astype(jnp.bfloat16)


def block_start(owner, count, tokens):
    return jnp.minimum(owner * count, tokens - count)


def time_kernel(devices, frames, info, *refs):
    sources = refs[:devices]
    gain_ref, weight_ref = refs[devices : devices + 2]
    outs = refs[devices + 2 : 2 * devices + 2]
    normed_ref, qkv_ref, att_ref, bias_ref = refs[2 * devices + 2 :]
    half = devices * frames * 8
    group = frames * 8

    @pl.when(pl.program_id(0) == 0)
    def _():
        row = lax.broadcasted_iota(jnp.int32, (half, half), 0)
        col = lax.broadcasted_iota(jnp.int32, (half, half), 1)
        source = info[1] - col // group
        source = jnp.where(source < 0, source + devices, source)
        frame = source * frames + (col // 8) % frames
        valid = (row % 8 == col % 8) & (frame < info[2])
        bias_ref[...] = jnp.where(valid, 0.0, NEG).astype(jnp.float32)

    gain = gain_ref[...]
    for k, ref in enumerate(sources):
        values = ref[0] if k == 0 else ref[...]
        normed = values.astype(jnp.float32)
        for s in range(ROWS // 8):
            piece = normed[:, s * 8 : s * 8 + 8, :].reshape(group, normed.shape[-1])
            normed_ref[s * half + k * group : s * half + (k + 1) * group, :] = normalise(piece, gain)
    project_heads(normed_ref[...], weight_ref, qkv_ref)
    for s in range(ROWS // 8):
        attend(qkv_ref, pl.ds(s * half, half), bias_ref[...], att_ref)
    for k, ref in enumerate(outs):
        pieces = [
            att_ref[s * half + k * group : s * half + (k + 1) * group, :].astype(jnp.float32).reshape(frames, 8, HW)
            for s in range(ROWS // 8)
        ]
        ref[...] = jnp.concatenate(pieces, axis=1).astype(jnp.bfloat16)


def time_step(info, tokens, received, gain, weight, count):
    _, frames, _, width = tokens.shape
    devices = len(received) + 1
    rows = devices * frames * ROWS
    half = devices * frames * 8
    piece = pl.BlockSpec((frames, ROWS, width), lambda i, info: (0, i, 0))
    own = pl.BlockSpec((1, frames, ROWS, width), lambda i, info: (info[0], 0, info[3] + i, 0))
    whole = lambda a: pl.BlockSpec(a.shape, lambda i, info: (0,) * a.ndim)
    return pl.pallas_call(
        functools.partial(time_kernel, devices, frames),
        grid_spec=pltpu.PrefetchScalarGridSpec(
            num_scalar_prefetch=1,
            grid=(count // ROWS,),
            in_specs=[own] + [piece] * (devices - 1) + [whole(gain), whole(weight)],
            out_specs=[pl.BlockSpec((frames, ROWS, HW), lambda i, info: (0, i, 0))] * devices,
            scratch_shapes=[
                pltpu.VMEM((rows, width), jnp.bfloat16),
                pltpu.VMEM((rows, 3 * HW), jnp.bfloat16),
                pltpu.VMEM((rows, HW), jnp.bfloat16),
                pltpu.VMEM((half, half), jnp.float32),
            ],
        ),
        out_shape=[jax.ShapeDtypeStruct((frames, count, HW), jnp.bfloat16)] * devices,
        compiler_params=pltpu.CompilerParams(vmem_limit_bytes=VMEM_LIMIT),
        cost_estimate=pl.CostEstimate(
            flops=2 * count * devices * frames * width * 3 * HW, bytes_accessed=12_000_000, transcendentals=0
        ),
        name="time_attention",
    )(info, tokens, *received, gain, weight)


def space_kernel(devices, frames, count, aliased, info, x_ref, *refs):
    pieces = refs[:devices]
    time_out_ref, gain_ref, weight_ref, space_out_ref = refs[devices : devices + 4]
    refs = refs[devices + 4 + aliased :]
    out_ref, att_ref, mid_ref, qkv_ref = refs
    tokens = x_ref.shape[2]
    live = info[4] + info[5] + pl.program_id(0) < info[2]

    @pl.when(live)
    def _():
        for k, ref in enumerate(pieces):
            owner = info[1] + k
            owner = jnp.where(owner >= devices, owner - devices, owner)
            start = pl.multiple_of(block_start(owner, count, tokens), ROWS)
            att_ref[pl.ds(start, count), :] = ref[0]
        mid = x_ref[0, 0].astype(jnp.float32) + jnp.dot(
            att_ref[...], time_out_ref[...], preferred_element_type=jnp.float32
        )
        mid_ref[...] = mid.astype(jnp.bfloat16)
        project_heads(normalise(mid_ref[...].astype(jnp.float32), gain_ref[...]), weight_ref, qkv_ref)
        bias = jnp.where(lax.broadcasted_iota(jnp.int32, (1, tokens), 1) < info[3], 0.0, NEG).astype(jnp.float32)
        attend(qkv_ref, pl.ds(0, tokens), bias, att_ref)
        result = mid_ref[...].astype(jnp.float32) + jnp.dot(
            att_ref[...], space_out_ref[...], preferred_element_type=jnp.float32
        )
        keep = lax.broadcasted_iota(jnp.int32, (tokens, 1), 0) < info[3]
        out_ref[0, 0] = jnp.where(keep, result, 0.0).astype(jnp.bfloat16)

    @pl.when(jnp.logical_not(live))
    def _():
        out_ref[...] = jnp.zeros_like(out_ref)


def space_step(info, tokens, pieces, first, time_out, gain, weight, space_out, partial):
    _, _, places, width = tokens.shape
    devices = len(pieces)
    calls, count, _ = pieces[0].shape
    unit = pl.BlockSpec((1, 1, places, width), lambda i, info: (info[0], first + i, 0, 0))
    whole = lambda a: pl.BlockSpec(a.shape, lambda i, info: (0,) * a.ndim)
    aliased = partial is not None
    operands = [info, tokens, *pieces, time_out, gain, weight, space_out] + ([partial] if aliased else [])
    return pl.pallas_call(
        functools.partial(space_kernel, devices, calls, count, int(aliased)),
        grid_spec=pltpu.PrefetchScalarGridSpec(
            num_scalar_prefetch=1,
            grid=(calls,),
            in_specs=[unit]
            + [pl.BlockSpec((1, count, HW), lambda i, info: (i, 0, 0))] * devices
            + [whole(a) for a in (time_out, gain, weight, space_out)]
            + ([ANY] if aliased else []),
            out_specs=unit,
            scratch_shapes=[
                pltpu.VMEM((places, HW), jnp.bfloat16),
                pltpu.VMEM((places, width), jnp.bfloat16),
                pltpu.VMEM((places, 3 * HW), jnp.bfloat16),
            ],
        ),
        out_shape=jax.ShapeDtypeStruct(tokens.shape, jnp.bfloat16),
        input_output_aliases={len(operands) - 1: 0} if aliased else {},
        compiler_params=pltpu.CompilerParams(vmem_limit_bytes=VMEM_LIMIT),
        cost_estimate=pl.CostEstimate(
            flops=2 * calls * places * width * 5 * HW, bytes_accessed=8_000_000, transcendentals=0
        ),
        name="space_block",
    )(*operands)


def pack_kernel(devices, count, info, x_ref, *refs):
    outs = refs[: devices - 1]
    sems = refs[-1]
    tokens = x_ref.shape[2]
    copies = []
    for k, ref in enumerate(outs):
        owner = info[1] + k + 1
        owner = jnp.where(owner >= devices, owner - devices, owner)
        start = pl.multiple_of(block_start(owner, count, tokens), ROWS)
        copies.append(pltpu.make_async_copy(x_ref.at[info[0], :, pl.ds(start, count), :], ref, sems.at[k]))
    for copy in copies:
        copy.start()
    for copy in copies:
        copy.wait()


def pack_step(info, tokens, devices, count):
    _, frames, _, width = tokens.shape
    return pl.pallas_call(
        functools.partial(pack_kernel, devices, count),
        in_specs=[pl.BlockSpec(memory_space=pltpu.SMEM), ANY],
        out_specs=[ANY] * (devices - 1),
        out_shape=[jax.ShapeDtypeStruct((frames, count, width), jnp.bfloat16)] * (devices - 1),
        scratch_shapes=[pltpu.SemaphoreType.DMA((devices - 1,))],
        name="pack_tokens",
    )(info, tokens)


def after(values, done):
    return lax.optimization_barrier((tuple(values), tuple(done)))


def send(blocks, devices, forward):
    results = []
    for k, block in enumerate(blocks, 1):
        pairs = [(i, (i + k) % devices) if forward else ((i + k) % devices, i) for i in range(devices)]
        results.append(lax.ppermute(block, "frame", pairs))
    return results


def per_device(
    devices,
    video_tokens,
    frame_count,
    token_count,
    time_gain,
    time_qkv,
    time_out,
    space_gain,
    space_qkv,
    space_out,
):
    clips, frames, places, width = video_tokens.shape
    count = places // devices
    me = lax.axis_index("frame").astype(jnp.int32)
    time_gain = time_gain[None, :]
    space_gain = space_gain[None, :]
    first_frame = me * frames
    start = block_start(me, count, places) // ROWS

    def time_info(c):
        return jnp.stack([jnp.int32(c), me, frame_count[c], start])

    def space_info(c, first):
        return jnp.stack([jnp.int32(c), me, frame_count[c], token_count[c], first_frame, jnp.int32(first)])

    sent_a = pack_step(time_info(0), video_tokens, devices, count)
    got_a = send(sent_a, devices, True)
    sent_b = pack_step(time_info(1), video_tokens, devices, count)
    got_b = []
    for k in range(devices - 1):
        (block,), (got_a[k],) = after([sent_b[k]], [got_a[k]])
        pairs = [(i, (i + k + 1) % devices) for i in range(devices)]
        got_b.append(lax.ppermute(block, "frame", pairs))
    att_a = time_step(time_info(0), video_tokens, got_a, time_gain, time_qkv, count)
    back_a = [att_a[0]]
    for k in range(devices - 1):
        (block,), (got_b[k],) = after([att_a[k + 1]], [got_b[k]])
        pairs = [((i + k + 1) % devices, i) for i in range(devices)]
        back_a.append(lax.ppermute(block, "frame", pairs))
    att_b = time_step(time_info(1), video_tokens, got_b, time_gain, time_qkv, count)
    halves = [(0, frames // 2), (frames // 2, frames)]
    back_b = []
    for first, last in halves:
        blocks = [a[first:last] for a in att_b]
        back_b.append([blocks[0]] + send(blocks[1:], devices, False))
    weights = (time_out, space_gain, space_qkv, space_out)
    out = space_step(space_info(0, 0), video_tokens, back_a, 0, *weights, None)
    for (first, _), pieces in zip(halves, back_b):
        out = space_step(space_info(1, first), video_tokens, pieces, first, *weights, out)
    return out


def solution(mesh):
    placed = (P("clip", "frame", None, None), P("clip"), P("clip"), P(), P(), P(), P(), P(), P())
    return jax.shard_map(
        functools.partial(per_device, mesh.shape["frame"]),
        mesh=mesh,
        in_specs=placed,
        out_specs=P("clip", "frame", None, None),
        check_vma=False,
    )
```

profile of v0, /device:TPU:0, one launch (start us, length us, event | category | flops | bytes accessed | tf_op | source)
XLA Modules:
  0.0 280.7 jit_solution(5357183561393202269)
XLA Ops:
  0.0 1.4 fusion.9
  1.4 1.9 add_add_fusion
  3.3 57.6 %pack_tokens.3 = (bf16[4,32,1024]{2,1,0:T(8,128)(2,1)}, bf16[4,32,1024]{2,1,0:T(8,128)(2,1)}, bf16[4,32,1024]{2,1,0:T(8,128)(2,1)}, bf16[4,32,1024]{2,1,0:T(8,12...) custom-call(s32[4]{0:T(128)} %get-tuple-element.142.info, ...), custom_call_target="tpu_custom_call" | custom-call | tf_op jit(solution)/shard_map/pack_tokens/pallas_call | solution.py:208
  60.8 3.0 %collective-permute-start = (bf16[4,32,1024]{2,1,0:T(8,128)(2,1)}, bf16[4,32,1024]{2,1,0:T(8,128)(2,1)S(1)}, u32[]{:S(2)}, u32[]{:S(2)}) collective-permute-start(bf16[4,32,1024]{2,1,0:T(8,128)(2,1)} %get-tuple-element.64), channel_id=1, source_target_pairs={{0,1},{1,2},{2,3},{3,4},{4,5},{5,6},{6,7},{7,0},{8,9},{9,10},{10,1... | collective-permute-start | bytes 786440 | tf_op jit(solution)/shard_map/ppermute | solution.py:226
  63.9 1.6 collective-permute-start.1
  65.4 2.5 collective-permute-start.2
  69.2 2.6 collective-permute-start.4
  71.9 57.4 %pack_tokens.2 = (bf16[4,32,1024]{2,1,0:T(8,128)(2,1)}, bf16[4,32,1024]{2,1,0:T(8,128)(2,1)}, bf16[4,32,1024]{2,1,0:T(8,128)(2,1)}, bf16[4,32,1024]{2,1,0:T(8,12...) custom-call(s32[4]{0:T(128)} %get-tuple-element.141.info, ...), custom_call_target="tpu_custom_call" | custom-call | tf_op jit(solution)/shard_map/pack_tokens/pallas_call | solution.py:208
  129.3 1.4 collective-permute-start.5
  130.7 1.4 collective-permute-start.6
  135.2 1.4 stack.43.info
  136.6 1.4 stack.18.info
  139.2 3.5 %collective-permute-start.10 = (bf16[4,32,1024]{2,1,0:T(8,128)(2,1)}, bf16[4,32,1024]{2,1,0:T(8,128)(2,1)S(1)}, u32[]{:S(2)}, u32[]{:S(2)}) collective-permute-start(bf16[4,32,1024]{2,1,0:T(8,128)(2,1)} %get-tuple-element.94), channel_id=1, source_target_pairs={{0,4},{1,5},{2,6},{3,7},{4,0},{5,1},{6,2},{7,3},{8,12},{9,13},{10,... | collective-permute-start | bytes 786440 | tf_op jit(solution)/shard_map/ppermute | solution.py:263
  143.1 2.3 collective-permute-start.11
  145.5 20.8 %collective-permute-start.12 = (bf16[4,32,1024]{2,1,0:T(8,128)(2,1)}, bf16[4,32,1024]{2,1,0:T(8,128)(2,1)S(1)}, u32[]{:S(2)}, u32[]{:S(2)}) collective-permute-start(bf16[4,32,1024]{2,1,0:T(8,128)(2,1)} %get-tuple-element.100), channel_id=1, source_target_pairs={{0,6},{1,7},{2,0},{3,1},{4,2},{5,3},{6,4},{7,5},{8,14},{9,15},{10,... | collective-permute-start | bytes 786440 | tf_op jit(solution)/shard_map/ppermute | solution.py:263
  166.3 11.8 %time_attention.2 = (bf16[4,32,512]{2,1,0:T(8,128)(2,1)S(1)}, bf16[4,32,512]{2,1,0:T(8,128)(2,1)S(1)}, bf16[4,32,512]{2,1,0:T(8,128)(2,1)S(1)}, bf16[4,32,512]{2...) custom-call(s32[4]{0:T(128)S(1)} %copy-done.4, ...), custom_call_target="tpu_custom_call" | custom-call | flops 3221225472 | bytes 12000000 | tf_op jit(solution)/shard_map/time_attention/pallas_call | solution.py:100
  178.2 8.8 %collective-permute-start.33 = (bf16[4,32,512]{2,1,0:T(8,128)(2,1)S(1)}, bf16[4,32,512]{2,1,0:T(8,128)(2,1)S(1)}, u32[]{:S(2)}, u32[]{:S(2)}) collective-permute-start(bf16[4,32,512]{2,1,0:T(8,128)(2,1)S(1)} %get-tuple-element.119), channel_id=1, source_target_pairs={{6,0},{7,1},{0,2},{1,3},{2,4},{3,5},{4,6},{5,7},{14,8},{15,9},{8,1... | collective-permute-start | bytes 393224 | tf_op jit(solution)/shard_map/ppermute | solution.py:269
  187.1 11.8 %time_attention.3 = (bf16[4,32,512]{2,1,0:T(8,128)(2,1)S(1)}, bf16[4,32,512]{2,1,0:T(8,128)(2,1)S(1)}, bf16[4,32,512]{2,1,0:T(8,128)(2,1)S(1)}, bf16[4,32,512]{2...) custom-call(s32[4]{0:T(128)S(1)} %copy-done.3, ...), custom_call_target="tpu_custom_call" | custom-call | flops 3221225472 | bytes 12000000 | tf_op jit(solution)/shard_map/time_attention/pallas_call | solution.py:100
  199.0 3.7 %collective-permute-start.21 = (bf16[2,32,512]{2,1,0:T(8,128)(2,1)S(1)}, bf16[2,32,512]{2,1,0:T(8,128)(2,1)S(1)}, u32[]{:S(2)}, u32[]{:S(2)}) collective-permute-start(bf16[2,32,512]{2,1,0:T(8,128)(2,1)S(1)} %get-tuple-element.133), channel_id=1, source_target_pairs={{1,0},{2,1},{3,2},{4,3},{5,4},{6,5},{7,6},{0,7},{9,8},{10,9},{11,1... | collective-permute-start | bytes 196616 | tf_op jit(solution)/shard_map/ppermute | solution.py:226
  202.8 3.8 %collective-permute-start.22 = (bf16[2,32,512]{2,1,0:T(8,128)(2,1)S(1)}, bf16[2,32,512]{2,1,0:T(8,128)(2,1)S(1)}, u32[]{:S(2)}, u32[]{:S(2)}) collective-permute-start(bf16[2,32,512]{2,1,0:T(8,128)(2,1)S(1)} %get-tuple-element.131), channel_id=1, source_target_pairs={{2,0},{3,1},{4,2},{5,3},{6,4},{7,5},{0,6},{1,7},{10,8},{11,9},{12,... | collective-permute-start | bytes 196616 | tf_op jit(solution)/shard_map/ppermute | solution.py:226
  206.7 2.4 collective-permute-start.15
  209.1 2.5 collective-permute-start.31
  211.7 2.2 collective-permute-start.30
  213.8 2.2 collective-permute-start.29
  216.1 4.8 %collective-permute-start.28 = (bf16[4,32,512]{2,1,0:T(8,128)(2,1)S(1)}, bf16[4,32,512]{2,1,0:T(8,128)(2,1)S(1)}, u32[]{:S(2)}, u32[]{:S(2)}) collective-permute-start(bf16[4,32,512]{2,1,0:T(8,128)(2,1)S(1)} %get-tuple-element.114), channel_id=1, source_target_pairs={{1,0},{2,1},{3,2},{4,3},{5,4},{6,5},{7,6},{0,7},{9,8},{10,9},{11,1... | collective-permute-start | bytes 393224 | tf_op jit(solution)/shard_map/ppermute | solution.py:269
  222.5 2.0 collective-permute-start.24
  224.5 10.6 %collective-permute-start.25 = (bf16[2,32,512]{2,1,0:T(8,128)(2,1)S(1)}, bf16[2,32,512]{2,1,0:T(8,128)(2,1)S(1)}, u32[]{:S(2)}, u32[]{:S(2)}) collective-permute-start(bf16[2,32,512]{2,1,0:T(8,128)(2,1)S(1)} %get-tuple-element.125), channel_id=1, source_target_pairs={{5,0},{6,1},{7,2},{0,3},{1,4},{2,5},{3,6},{4,7},{13,8},{14,9},{15,... | collective-permute-start | bytes 196616 | tf_op jit(solution)/shard_map/ppermute | solution.py:226
  235.8 16.2 %space_block.3.refs_12_ = bf16[2,4,256,1024]{3,2,1,0:T(8,128)(2,1)} custom-call(s32[6]{0:T(128)S(1)} %stack.44.info, bf16[2,4,256,1024]{3,2,1,0:T(8,128)(2,1)} %x_ref.9, bf16[4,32,512]{2,1,0:T(8,128)(2,1)S(1)} %get-tuple-element.113.refs_0_, bf16[4,32,512]{2,1,0:T(8,128)(2,1)S(1)} %collective-permute-done.28.refs_1_, ...), custom_call_target="tpu_custom_call" | custom-call | flops 5368709120 | bytes 8000000 | tf_op jit(solution)/shard_map/space_block/pallas_call | solution.py:164
  252.0 4.7 %collective-permute-start.16 = (bf16[2,32,512]{2,1,0:T(8,128)(2,1)S(1)}, bf16[2,32,512]{2,1,0:T(8,128)(2,1)S(1)}, u32[]{:S(2)}, u32[]{:S(2)}) collective-permute-start(bf16[2,32,512]{2,1,0:T(8,128)(2,1)S(1)} %get-tuple-element.130), channel_id=1, source_target_pairs={{3,0},{4,1},{5,2},{6,3},{7,4},{0,5},{1,6},{2,7},{11,8},{12,9},{13,... | collective-permute-start | bytes 196616 | tf_op jit(solution)/shard_map/ppermute | solution.py:226
  257.4 3.7 %collective-permute-start.20 = (bf16[2,32,512]{2,1,0:T(8,128)(2,1)S(1)}, bf16[2,32,512]{2,1,0:T(8,128)(2,1)S(1)}, u32[]{:S(2)}, u32[]{:S(2)}) collective-permute-start(bf16[2,32,512]{2,1,0:T(8,128)(2,1)S(1)} %get-tuple-element.122), channel_id=1, source_target_pairs={{7,0},{0,1},{1,2},{2,3},{3,4},{4,5},{5,6},{6,7},{15,8},{8,9},{9,10... | collective-permute-start | bytes 196616 | tf_op jit(solution)/shard_map/ppermute | solution.py:226
  261.1 9.8 %space_block.4.refs_12_ = bf16[2,4,256,1024]{3,2,1,0:T(8,128)(2,1)} custom-call(s32[6]{0:T(128)S(1)} %stack.43.info, bf16[2,4,256,1024]{3,2,1,0:T(8,128)(2,1)} %x_ref.9, bf16[2,32,512]{2,1,0:T(8,128)(2,1)S(1)} %get-tuple-element.135.refs_0_, bf16[2,32,512]{2,1,0:T(8,128)(2,1)S(1)} %collective-permute-done.21.refs_1_, ...), custom_call_target="tpu_custom_call", output_to_operand_aliasing={{}: (14, {})} | custom-call | flops 2684354560 | bytes 8000000 | tf_op jit(solution)/shard_map/space_block/pallas_call | solution.py:164
  270.9 9.8 %space_block.5 = bf16[2,4,256,1024]{3,2,1,0:T(8,128)(2,1)} custom-call(s32[6]{0:T(128)S(1)} %stack.18.info, bf16[2,4,256,1024]{3,2,1,0:T(8,128)(2,1)} %x_ref.9, bf16[2,32,512]{2,1,0:T(8,128)(2,1)S(1)} %get-tuple-element.136.refs_0_, bf16[2,32,512]{2,1,0:T(8,128)(2,1)S(1)} %collective-permute-done.14.refs_1_, ...), custom_call_target="tpu_custom_call", output_to_operand_aliasing={{}: (14, {})} | custom-call | flops 2684354560 | bytes 8000000 | tf_op jit(solution)/shard_map/space_block/pallas_call | solution.py:164
  (77 shorter events, 9.1 us)
Async XLA Ops:
  60.8 68.4 %collective-permute-start = (bf16[4,32,1024]{2,1,0:T(8,128)(2,1)}, bf16[4,32,1024]{2,1,0:T(8,128)(2,1)S(1)}, u32[]{:S(2)}, u32[]{:S(2)}) collective-permute-start(bf16[4,32,1024]{2,1,0:T(8,128)(2,1)} %get-tuple-element.64), channel_id=1, source_target_pairs={{0,1},{1,2},{2,3},{3,4},{4,5},{5,6},{6,7},{7,0},{8,9},{9,10},{10,1... | collective-permute-start | bytes 786440 | tf_op jit(solution)/shard_map/ppermute | solution.py:226
  63.9 66.8 %collective-permute-start.1 = (bf16[4,32,1024]{2,1,0:T(8,128)(2,1)}, bf16[4,32,1024]{2,1,0:T(8,128)(2,1)S(1)}, u32[]{:S(2)}, u32[]{:S(2)}) collective-permute-start(bf16[4,32,1024]{2,1,0:T(8,128)(2,1)} %get-tuple-element.67), channel_id=1, source_target_pairs={{0,2},{1,3},{2,4},{3,5},{4,6},{5,7},{6,0},{7,1},{8,10},{9,11},{10,... | collective-permute-start | bytes 786440 | tf_op jit(solution)/shard_map/ppermute | solution.py:226
  65.4 66.7 %collective-permute-start.2 = (bf16[4,32,1024]{2,1,0:T(8,128)(2,1)}, bf16[4,32,1024]{2,1,0:T(8,128)(2,1)S(1)}, u32[]{:S(2)}, u32[]{:S(2)}) collective-permute-start(bf16[4,32,1024]{2,1,0:T(8,128)(2,1)} %get-tuple-element.70), channel_id=1, source_target_pairs={{0,3},{1,4},{2,5},{3,6},{4,7},{5,0},{6,1},{7,2},{8,11},{9,12},{10,... | collective-permute-start | bytes 786440 | tf_op jit(solution)/shard_map/ppermute | solution.py:226
  68.0 64.8 %collective-permute-start.3 = (bf16[4,32,1024]{2,1,0:T(8,128)(2,1)}, bf16[4,32,1024]{2,1,0:T(8,128)(2,1)S(1)}, u32[]{:S(2)}, u32[]{:S(2)}) collective-permute-start(bf16[4,32,1024]{2,1,0:T(8,128)(2,1)} %get-tuple-element.73), channel_id=1, source_target_pairs={{0,4},{1,5},{2,6},{3,7},{4,0},{5,1},{6,2},{7,3},{8,12},{9,13},{10,... | collective-permute-start | bytes 786440 | tf_op jit(solution)/shard_map/ppermute | solution.py:226
  69.2 68.8 %collective-permute-start.4 = (bf16[4,32,1024]{2,1,0:T(8,128)(2,1)}, bf16[4,32,1024]{2,1,0:T(8,128)(2,1)S(1)}, u32[]{:S(2)}, u32[]{:S(2)}) collective-permute-start(bf16[4,32,1024]{2,1,0:T(8,128)(2,1)} %get-tuple-element.76), channel_id=1, source_target_pairs={{0,5},{1,6},{2,7},{3,0},{4,1},{5,2},{6,3},{7,4},{8,13},{9,14},{10,... | collective-permute-start | bytes 786440 | tf_op jit(solution)/shard_map/ppermute | solution.py:226
  129.3 9.9 %collective-permute-start.5 = (bf16[4,32,1024]{2,1,0:T(8,128)(2,1)S(1)}, bf16[4,32,1024]{2,1,0:T(8,128)(2,1)S(1)}, u32[]{:S(2)}, u32[]{:S(2)}) collective-permute-start(bf16[4,32,1024]{2,1,0:T(8,128)(2,1)S(1)} %copy-done.8), channel_id=1, source_target_pairs={{0,6},{1,7},{2,0},{3,1},{4,2},{5,3},{6,4},{7,5},{8,14},{9,15},{10,... | collective-permute-start | bytes 786440 | tf_op jit(solution)/shard_map/ppermute | solution.py:226
  130.7 12.4 %collective-permute-start.6 = (bf16[4,32,1024]{2,1,0:T(8,128)(2,1)S(1)}, bf16[4,32,1024]{2,1,0:T(8,128)(2,1)S(1)}, u32[]{:S(2)}, u32[]{:S(2)}) collective-permute-start(bf16[4,32,1024]{2,1,0:T(8,128)(2,1)S(1)} %copy-done.7), channel_id=1, source_target_pairs={{0,7},{1,0},{2,1},{3,2},{4,3},{5,4},{6,5},{7,6},{8,15},{9,8},{10,9... | collective-permute-start | bytes 786440 | tf_op jit(solution)/shard_map/ppermute | solution.py:226
  132.1 13.3 %collective-permute-start.7 = (bf16[4,32,1024]{2,1,0:T(8,128)(2,1)}, bf16[4,32,1024]{2,1,0:T(8,128)(2,1)S(1)}, u32[]{:S(2)}, u32[]{:S(2)}) collective-permute-start(bf16[4,32,1024]{2,1,0:T(8,128)(2,1)} %get-tuple-element.85), channel_id=1, source_target_pairs={{0,1},{1,2},{2,3},{3,4},{4,5},{5,6},{6,7},{7,0},{8,9},{9,10},{10,1... | collective-permute-start | bytes 786440 | tf_op jit(solution)/shard_map/ppermute | solution.py:263
  132.7 33.6 %collective-permute-start.8 = (bf16[4,32,1024]{2,1,0:T(8,128)(2,1)}, bf16[4,32,1024]{2,1,0:T(8,128)(2,1)S(1)}, u32[]{:S(2)}, u32[]{:S(2)}) collective-permute-start(bf16[4,32,1024]{2,1,0:T(8,128)(2,1)} %get-tuple-element.88), channel_id=1, source_target_pairs={{0,2},{1,3},{2,4},{3,5},{4,6},{5,7},{6,0},{7,1},{8,10},{9,11},{10,... | collective-permute-start | bytes 786440 | tf_op jit(solution)/shard_map/ppermute | solution.py:263
  138.0 40.2 %collective-permute-start.9 = (bf16[4,32,1024]{2,1,0:T(8,128)(2,1)}, bf16[4,32,1024]{2,1,0:T(8,128)(2,1)S(1)}, u32[]{:S(2)}, u32[]{:S(2)}) collective-permute-start(bf16[4,32,1024]{2,1,0:T(8,128)(2,1)} %get-tuple-element.91), channel_id=1, source_target_pairs={{0,3},{1,4},{2,5},{3,6},{4,7},{5,0},{6,1},{7,2},{8,11},{9,12},{10,... | collective-permute-start | bytes 786440 | tf_op jit(solution)/shard_map/ppermute | solution.py:263
  139.2 39.0 %collective-permute-start.10 = (bf16[4,32,1024]{2,1,0:T(8,128)(2,1)}, bf16[4,32,1024]{2,1,0:T(8,128)(2,1)S(1)}, u32[]{:S(2)}, u32[]{:S(2)}) collective-permute-start(bf16[4,32,1024]{2,1,0:T(8,128)(2,1)} %get-tuple-element.94), channel_id=1, source_target_pairs={{0,4},{1,5},{2,6},{3,7},{4,0},{5,1},{6,2},{7,3},{8,12},{9,13},{10,... | collective-permute-start | bytes 786440 | tf_op jit(solution)/shard_map/ppermute | solution.py:263
  143.1 35.1 %collective-permute-start.11 = (bf16[4,32,1024]{2,1,0:T(8,128)(2,1)}, bf16[4,32,1024]{2,1,0:T(8,128)(2,1)S(1)}, u32[]{:S(2)}, u32[]{:S(2)}) collective-permute-start(bf16[4,32,1024]{2,1,0:T(8,128)(2,1)} %get-tuple-element.97), channel_id=1, source_target_pairs={{0,5},{1,6},{2,7},{3,0},{4,1},{5,2},{6,3},{7,4},{8,13},{9,14},{10,... | collective-permute-start | bytes 786440 | tf_op jit(solution)/shard_map/ppermute | solution.py:263
  145.5 32.8 %collective-permute-start.12 = (bf16[4,32,1024]{2,1,0:T(8,128)(2,1)}, bf16[4,32,1024]{2,1,0:T(8,128)(2,1)S(1)}, u32[]{:S(2)}, u32[]{:S(2)}) collective-permute-start(bf16[4,32,1024]{2,1,0:T(8,128)(2,1)} %get-tuple-element.100), channel_id=1, source_target_pairs={{0,6},{1,7},{2,0},{3,1},{4,2},{5,3},{6,4},{7,5},{8,14},{9,15},{10,... | collective-permute-start | bytes 786440 | tf_op jit(solution)/shard_map/ppermute | solution.py:263
  166.3 20.7 %collective-permute-start.13 = (bf16[4,32,1024]{2,1,0:T(8,128)(2,1)}, bf16[4,32,1024]{2,1,0:T(8,128)(2,1)S(1)}, u32[]{:S(2)}, u32[]{:S(2)}) collective-permute-start(bf16[4,32,1024]{2,1,0:T(8,128)(2,1)} %get-tuple-element.103), channel_id=1, source_target_pairs={{0,7},{1,0},{2,1},{3,2},{4,3},{5,4},{6,5},{7,6},{8,15},{9,8},{10,9... | collective-permute-start | bytes 786440 | tf_op jit(solution)/shard_map/ppermute | solution.py:263
  178.2 37.9 %collective-permute-start.33 = (bf16[4,32,512]{2,1,0:T(8,128)(2,1)S(1)}, bf16[4,32,512]{2,1,0:T(8,128)(2,1)S(1)}, u32[]{:S(2)}, u32[]{:S(2)}) collective-permute-start(bf16[4,32,512]{2,1,0:T(8,128)(2,1)S(1)} %get-tuple-element.119), channel_id=1, source_target_pairs={{6,0},{7,1},{0,2},{1,3},{2,4},{3,5},{4,6},{5,7},{14,8},{15,9},{8,1... | collective-permute-start | bytes 393224 | tf_op jit(solution)/shard_map/ppermute | solution.py:269
  187.0 33.8 %collective-permute-start.32 = (bf16[4,32,512]{2,1,0:T(8,128)(2,1)S(1)}, bf16[4,32,512]{2,1,0:T(8,128)(2,1)S(1)}, u32[]{:S(2)}, u32[]{:S(2)}) collective-permute-start(bf16[4,32,512]{2,1,0:T(8,128)(2,1)S(1)} %get-tuple-element.118), channel_id=1, source_target_pairs={{5,0},{6,1},{7,2},{0,3},{1,4},{2,5},{3,6},{4,7},{13,8},{14,9},{15,... | collective-permute-start | bytes 393224 | tf_op jit(solution)/shard_map/ppermute | solution.py:269
  202.8 8.9 %collective-permute-start.22 = (bf16[2,32,512]{2,1,0:T(8,128)(2,1)S(1)}, bf16[2,32,512]{2,1,0:T(8,128)(2,1)S(1)}, u32[]{:S(2)}, u32[]{:S(2)}) collective-permute-start(bf16[2,32,512]{2,1,0:T(8,128)(2,1)S(1)} %get-tuple-element.131), channel_id=1, source_target_pairs={{2,0},{3,1},{4,2},{5,3},{6,4},{7,5},{0,6},{1,7},{10,8},{11,9},{12,... | collective-permute-start | bytes 196616 | tf_op jit(solution)/shard_map/ppermute | solution.py:226
  209.1 13.0 %collective-permute-start.31 = (bf16[4,32,512]{2,1,0:T(8,128)(2,1)S(1)}, bf16[4,32,512]{2,1,0:T(8,128)(2,1)S(1)}, u32[]{:S(2)}, u32[]{:S(2)}) collective-permute-start(bf16[4,32,512]{2,1,0:T(8,128)(2,1)S(1)} %get-tuple-element.117), channel_id=1, source_target_pairs={{4,0},{5,1},{6,2},{7,3},{0,4},{1,5},{2,6},{3,7},{12,8},{13,9},{14,... | collective-permute-start | bytes 393224 | tf_op jit(solution)/shard_map/ppermute | solution.py:269
  211.7 10.8 %collective-permute-start.30 = (bf16[4,32,512]{2,1,0:T(8,128)(2,1)S(1)}, bf16[4,32,512]{2,1,0:T(8,128)(2,1)S(1)}, u32[]{:S(2)}, u32[]{:S(2)}) collective-permute-start(bf16[4,32,512]{2,1,0:T(8,128)(2,1)S(1)} %get-tuple-element.116), channel_id=1, source_target_pairs={{3,0},{4,1},{5,2},{6,3},{7,4},{0,5},{1,6},{2,7},{11,8},{12,9},{13,... | collective-permute-start | bytes 393224 | tf_op jit(solution)/shard_map/ppermute | solution.py:269
  213.8 10.6 %collective-permute-start.29 = (bf16[4,32,512]{2,1,0:T(8,128)(2,1)S(1)}, bf16[4,32,512]{2,1,0:T(8,128)(2,1)S(1)}, u32[]{:S(2)}, u32[]{:S(2)}) collective-permute-start(bf16[4,32,512]{2,1,0:T(8,128)(2,1)S(1)} %get-tuple-element.115), channel_id=1, source_target_pairs={{2,0},{3,1},{4,2},{5,3},{6,4},{7,5},{0,6},{1,7},{10,8},{11,9},{12,... | collective-permute-start | bytes 393224 | tf_op jit(solution)/shard_map/ppermute | solution.py:269
  216.1 19.0 %collective-permute-start.28 = (bf16[4,32,512]{2,1,0:T(8,128)(2,1)S(1)}, bf16[4,32,512]{2,1,0:T(8,128)(2,1)S(1)}, u32[]{:S(2)}, u32[]{:S(2)}) collective-permute-start(bf16[4,32,512]{2,1,0:T(8,128)(2,1)S(1)} %get-tuple-element.114), channel_id=1, source_target_pairs={{1,0},{2,1},{3,2},{4,3},{5,4},{6,5},{7,6},{0,7},{9,8},{10,9},{11,1... | collective-permute-start | bytes 393224 | tf_op jit(solution)/shard_map/ppermute | solution.py:269
  220.9 14.4 %collective-permute-start.34 = (bf16[4,32,512]{2,1,0:T(8,128)(2,1)S(1)}, bf16[4,32,512]{2,1,0:T(8,128)(2,1)S(1)}, u32[]{:S(2)}, u32[]{:S(2)}) collective-permute-start(bf16[4,32,512]{2,1,0:T(8,128)(2,1)S(1)} %get-tuple-element.120), channel_id=1, source_target_pairs={{7,0},{0,1},{1,2},{2,3},{3,4},{4,5},{5,6},{6,7},{15,8},{8,9},{9,10... | collective-permute-start | bytes 393224 | tf_op jit(solution)/shard_map/ppermute | solution.py:269
  222.1 29.9 %collective-permute-start.23 = (bf16[2,32,512]{2,1,0:T(8,128)(2,1)S(1)}, bf16[2,32,512]{2,1,0:T(8,128)(2,1)S(1)}, u32[]{:S(2)}, u32[]{:S(2)}) collective-permute-start(bf16[2,32,512]{2,1,0:T(8,128)(2,1)S(1)} %get-tuple-element.129), channel_id=1, source_target_pairs={{3,0},{4,1},{5,2},{6,3},{7,4},{0,5},{1,6},{2,7},{11,8},{12,9},{13,... | collective-permute-start | bytes 196616 | tf_op jit(solution)/shard_map/ppermute | solution.py:226
  222.5 34.2 %collective-permute-start.24 = (bf16[2,32,512]{2,1,0:T(8,128)(2,1)S(1)}, bf16[2,32,512]{2,1,0:T(8,128)(2,1)S(1)}, u32[]{:S(2)}, u32[]{:S(2)}) collective-permute-start(bf16[2,32,512]{2,1,0:T(8,128)(2,1)S(1)} %get-tuple-element.127), channel_id=1, source_target_pairs={{4,0},{5,1},{6,2},{7,3},{0,4},{1,5},{2,6},{3,7},{12,8},{13,9},{14,... | collective-permute-start | bytes 196616 | tf_op jit(solution)/shard_map/ppermute | solution.py:226
  224.5 32.2 %collective-permute-start.25 = (bf16[2,32,512]{2,1,0:T(8,128)(2,1)S(1)}, bf16[2,32,512]{2,1,0:T(8,128)(2,1)S(1)}, u32[]{:S(2)}, u32[]{:S(2)}) collective-permute-start(bf16[2,32,512]{2,1,0:T(8,128)(2,1)S(1)} %get-tuple-element.125), channel_id=1, source_target_pairs={{5,0},{6,1},{7,2},{0,3},{1,4},{2,5},{3,6},{4,7},{13,8},{14,9},{15,... | collective-permute-start | bytes 196616 | tf_op jit(solution)/shard_map/ppermute | solution.py:226
  235.1 21.6 %collective-permute-start.26 = (bf16[2,32,512]{2,1,0:T(8,128)(2,1)S(1)}, bf16[2,32,512]{2,1,0:T(8,128)(2,1)S(1)}, u32[]{:S(2)}, u32[]{:S(2)}) collective-permute-start(bf16[2,32,512]{2,1,0:T(8,128)(2,1)S(1)} %get-tuple-element.123), channel_id=1, source_target_pairs={{6,0},{7,1},{0,2},{1,3},{2,4},{3,5},{4,6},{5,7},{14,8},{15,9},{8,1... | collective-permute-start | bytes 196616 | tf_op jit(solution)/shard_map/ppermute | solution.py:226
  235.2 22.1 %collective-permute-start.27 = (bf16[2,32,512]{2,1,0:T(8,128)(2,1)S(1)}, bf16[2,32,512]{2,1,0:T(8,128)(2,1)S(1)}, u32[]{:S(2)}, u32[]{:S(2)}) collective-permute-start(bf16[2,32,512]{2,1,0:T(8,128)(2,1)S(1)} %get-tuple-element.121), channel_id=1, source_target_pairs={{7,0},{0,1},{1,2},{2,3},{3,4},{4,5},{5,6},{6,7},{15,8},{8,9},{9,10... | collective-permute-start | bytes 196616 | tf_op jit(solution)/shard_map/ppermute | solution.py:226
  252.0 18.9 %collective-permute-start.16 = (bf16[2,32,512]{2,1,0:T(8,128)(2,1)S(1)}, bf16[2,32,512]{2,1,0:T(8,128)(2,1)S(1)}, u32[]{:S(2)}, u32[]{:S(2)}) collective-permute-start(bf16[2,32,512]{2,1,0:T(8,128)(2,1)S(1)} %get-tuple-element.130), channel_id=1, source_target_pairs={{3,0},{4,1},{5,2},{6,3},{7,4},{0,5},{1,6},{2,7},{11,8},{12,9},{13,... | collective-permute-start | bytes 196616 | tf_op jit(solution)/shard_map/ppermute | solution.py:226
  256.6 14.2 %collective-permute-start.17 = (bf16[2,32,512]{2,1,0:T(8,128)(2,1)S(1)}, bf16[2,32,512]{2,1,0:T(8,128)(2,1)S(1)}, u32[]{:S(2)}, u32[]{:S(2)}) collective-permute-start(bf16[2,32,512]{2,1,0:T(8,128)(2,1)S(1)} %get-tuple-element.128), channel_id=1, source_target_pairs={{4,0},{5,1},{6,2},{7,3},{0,4},{1,5},{2,6},{3,7},{12,8},{13,9},{14,... | collective-permute-start | bytes 196616 | tf_op jit(solution)/shard_map/ppermute | solution.py:226
  256.7 14.2 %collective-permute-start.18 = (bf16[2,32,512]{2,1,0:T(8,128)(2,1)S(1)}, bf16[2,32,512]{2,1,0:T(8,128)(2,1)S(1)}, u32[]{:S(2)}, u32[]{:S(2)}) collective-permute-start(bf16[2,32,512]{2,1,0:T(8,128)(2,1)S(1)} %get-tuple-element.126), channel_id=1, source_target_pairs={{5,0},{6,1},{7,2},{0,3},{1,4},{2,5},{3,6},{4,7},{13,8},{14,9},{15,... | collective-permute-start | bytes 196616 | tf_op jit(solution)/shard_map/ppermute | solution.py:226
  256.7 14.2 %collective-permute-start.19 = (bf16[2,32,512]{2,1,0:T(8,128)(2,1)S(1)}, bf16[2,32,512]{2,1,0:T(8,128)(2,1)S(1)}, u32[]{:S(2)}, u32[]{:S(2)}) collective-permute-start(bf16[2,32,512]{2,1,0:T(8,128)(2,1)S(1)} %get-tuple-element.124), channel_id=1, source_target_pairs={{6,0},{7,1},{0,2},{1,3},{2,4},{3,5},{4,6},{5,7},{14,8},{15,9},{8,1... | collective-permute-start | bytes 196616 | tf_op jit(solution)/shard_map/ppermute | solution.py:226
  257.4 13.5 %collective-permute-start.20 = (bf16[2,32,512]{2,1,0:T(8,128)(2,1)S(1)}, bf16[2,32,512]{2,1,0:T(8,128)(2,1)S(1)}, u32[]{:S(2)}, u32[]{:S(2)}) collective-permute-start(bf16[2,32,512]{2,1,0:T(8,128)(2,1)S(1)} %get-tuple-element.122), channel_id=1, source_target_pairs={{7,0},{0,1},{1,2},{2,3},{3,4},{4,5},{5,6},{6,7},{15,8},{8,9},{9,10... | collective-permute-start | bytes 196616 | tf_op jit(solution)/shard_map/ppermute | solution.py:226
  (12 other events, 782.6 us)
where the time goes:
time: 281 us
  Pallas kernels  174 us (62%)
  starting transfers between devices  96.3 us (34%)
  local copies, waits for them, and re-layouts  6.09 us (2%)
    pallas_call x2, Pallas kernels, pack_step(): pl.pallas_call(functools.partial(pack_kernel, devices, count), in_specs=[...  115 us
    ppermute x21, starting transfers between devices, send(): results.append(lax.ppermute(block, 'frame', pairs))  46.6 us
    pallas_call x3, Pallas kernels, space_step(): pl.pallas_call(functools.partial(space_kernel, devices, calls, count, int...  35.8 us
    ppermute x7, starting transfers between devices, per_device(): got_b.append(lax.ppermute(block, 'frame', pairs))  29.2 us
    pallas_call x2, Pallas kernels, time_step(): pl.pallas_call(functools.partial(time_kernel, devices, frames), grid_spec...  23.7 us
    ppermute x7, starting transfers between devices, per_device(): back_a.append(lax.ppermute(block, 'frame', pairs))  20.5 us
  transfers between devices with their start and end apart: 35, of which 2 were waited for; matrix products, arithmetic and copies ran while one was open for 2% of the time, Pallas kernels for 38%

commit v1 on v0

v1 whole, which is shorter than its diff:
```python
import functools

import jax
import jax.numpy as jnp
from jax import lax
from jax.experimental import pallas as pl
from jax.experimental.pallas import tpu as pltpu
from jax.sharding import PartitionSpec as P

HEADS = 8
HD = 64
HW = 512
ROWS = 16
NEG = -1e30
AHEAD = 0
BEHIND = 0
VMEM_LIMIT = 50 * 1024 * 1024
def KEPT(a):
    return pl.BlockSpec(a.shape, lambda i, *_: (0,) * a.ndim)


ANY = pl.BlockSpec(memory_space=pl.ANY)


def normalise(values, gain):
    centre = values - jnp.mean(values, axis=-1, keepdims=True)
    spread = jnp.mean(centre * centre, axis=-1, keepdims=True)
    return (centre * lax.rsqrt(spread + 1e-05) * gain).astype(jnp.bfloat16)


def attend(qkv_ref, rows, bias, out_ref):
    count = rows.size
    low = lax.broadcasted_iota(jnp.int32, (count, 2 * HD), 1) < HD
    zero = jnp.zeros((count, 2 * HD), jnp.bfloat16)
    for pair in range(HEADS // 2):
        cols = pair * 2 * HD
        q = qkv_ref[rows, cols : cols + 2 * HD]
        k = qkv_ref[rows, HW + cols : HW + cols + 2 * HD]
        v = qkv_ref[rows, 2 * HW + cols : 2 * HW + cols + 2 * HD]
        parts = []
        for keys in (jnp.where(low, k, zero), jnp.where(low, zero, k)):
            scores = lax.dot_general(q, keys, (((1,), (1,)), ((), ())), preferred_element_type=jnp.float32)
            scores = scores + bias
            expo = jnp.exp(scores - jnp.max(scores, axis=-1, keepdims=True))
            weights = (expo * (1.0 / jnp.sum(expo, axis=-1, keepdims=True))).astype(jnp.bfloat16)
            parts.append(jnp.dot(weights, v, preferred_element_type=jnp.float32))
        out_ref[rows, cols : cols + 2 * HD] = jnp.where(low, parts[0], parts[1]).astype(jnp.bfloat16)


def project_heads(normed, weight_ref, qkv_ref):
    for part in range(3):
        result = jnp.dot(normed, weight_ref[:, part * HW : (part + 1) * HW], preferred_element_type=jnp.float32)
        if part == 0:
            result = result * HD ** (-0.5)
        qkv_ref[:, part * HW : (part + 1) * HW] = result.astype(jnp.bfloat16)


def clip_at(slot, frame_count):
    return jnp.where(frame_count[1] > frame_count[0], 1 - slot, slot)


def block_start(owner, count, tokens):
    return jnp.minimum(owner * count, tokens - count)


class Route:
    def __init__(self, whole, devices, count):
        self.whole, self.devices, self.count = whole, devices, count

    def peer(self, me, k):
        return k if self.whole else me ^ k


def time_kernel(route, frames, slot, frame_count, *refs):
    devices = route.devices
    n_in = 1 if route.whole else devices
    sources = refs[:n_in]
    gain_ref, weight_ref = refs[n_in : n_in + 2]
    outs = refs[n_in + 2 : -4]
    normed_ref, qkv_ref, att_ref, bias_ref = refs[-4:]
    half = devices * frames * 8
    group = frames * 8
    me = lax.axis_index("frame")

    @pl.when(pl.program_id(0) == 0)
    def _():
        row = lax.broadcasted_iota(jnp.int32, (half, half), 0)
        col = lax.broadcasted_iota(jnp.int32, (half, half), 1)
        frame = route.peer(me, col // group) * frames + (col // 8) % frames
        valid = (row % 8 == col % 8) & (frame < frame_count[clip_at(slot, frame_count)])
        bias_ref[...] = jnp.where(valid, 0.0, NEG).astype(jnp.float32)

    gain = gain_ref[...]
    for k in range(devices):
        if route.whole:
            values = sources[0][k]
        else:
            values = sources[0][0] if k == 0 else sources[k][...]
        normed = values.astype(jnp.float32)
        for s in range(ROWS // 8):
            piece = normed[:, s * 8 : s * 8 + 8, :].reshape(group, normed.shape[-1])
            normed_ref[s * half + k * group : s * half + (k + 1) * group, :] = normalise(piece, gain)
    project_heads(normed_ref[...], weight_ref, qkv_ref)
    for s in range(ROWS // 8):
        attend(qkv_ref, pl.ds(s * half, half), bias_ref[...], att_ref)
    for k in range(devices):
        pieces = [
            att_ref[s * half + k * group : s * half + (k + 1) * group, :].astype(jnp.float32).reshape(frames, 8, HW)
            for s in range(ROWS // 8)
        ]
        result = jnp.concatenate(pieces, axis=1).astype(jnp.bfloat16)
        if route.whole:
            outs[0][k] = result
        else:
            early = outs[k].shape[0]
            outs[k][...] = result[:early]
            outs[-1][route.peer(me, k)] = result[early:]


def time_step(route, slot, frame_count, tokens, received, gain, weight, early=0):
    _, frames, places, width = tokens.shape
    devices, count = route.devices, route.count
    rows = devices * frames * ROWS
    half = devices * frames * 8

    def own_block(i, counts):
        start = block_start(lax.axis_index("frame"), count, places)
        return clip_at(slot, counts), 0, start // ROWS + i, 0

    if route.whole:
        operands = [received]
        in_specs = [pl.BlockSpec((devices, frames, ROWS, width), lambda i, *_: (0, 0, i, 0))]
        out_specs = [pl.BlockSpec((devices, frames, ROWS, HW), lambda i, *_: (0, 0, i, 0))]
        out_shape = [jax.ShapeDtypeStruct((devices, frames, count, HW), jnp.bfloat16)]
    else:
        operands = [tokens, *received]
        in_specs = [pl.BlockSpec((1, frames, ROWS, width), own_block)]
        in_specs += [pl.BlockSpec((frames, ROWS, width), lambda i, *_: (0, i, 0))] * (devices - 1)
        late = frames - early
        out_specs = [pl.BlockSpec((early, ROWS, HW), lambda i, *_: (0, i, 0))] * devices
        out_specs += [pl.BlockSpec((devices, late, ROWS, HW), lambda i, *_: (0, 0, i, 0))]
        out_shape = [jax.ShapeDtypeStruct((early, count, HW), jnp.bfloat16)] * devices
        out_shape += [jax.ShapeDtypeStruct((devices, late, count, HW), jnp.bfloat16)]
    return pl.pallas_call(
        functools.partial(time_kernel, route, frames, slot),
        grid_spec=pltpu.PrefetchScalarGridSpec(
            num_scalar_prefetch=1,
            grid=(count // ROWS,),
            in_specs=in_specs + [KEPT(gain), KEPT(weight)],
            out_specs=out_specs,
            scratch_shapes=[
                pltpu.VMEM((rows, width), jnp.bfloat16),
                pltpu.VMEM((rows, 3 * HW), jnp.bfloat16),
                pltpu.VMEM((rows, HW), jnp.bfloat16),
                pltpu.VMEM((half, half), jnp.float32),
            ],
        ),
        out_shape=out_shape,
        compiler_params=pltpu.CompilerParams(vmem_limit_bytes=VMEM_LIMIT),
        cost_estimate=pl.CostEstimate(
            flops=4 * count * devices * frames * width * 3 * HW, bytes_accessed=12_000_000, transcendentals=0
        ),
        name="time_attention",
    )(frame_count, *operands, gain, weight)


def space_kernel(route, frames, slot, first, aliased, frame_count, token_count, x_ref, *refs):
    devices, count = route.devices, route.count
    n_in = 1 if route.whole else devices
    pieces = refs[:n_in]
    gain_ref, time_out_ref, weight_ref, space_out_ref = refs[n_in : n_in + 4]
    out_ref, att_ref, mid_ref, qkv_ref = refs[n_in + 4 + aliased :]
    tokens = x_ref.shape[2]
    me = lax.axis_index("frame")
    clip = clip_at(slot, frame_count)
    token_end = token_count[clip]
    live = me * frames + first + pl.program_id(0) < frame_count[clip]

    @pl.when(live)
    def _():
        for k in range(devices):
            start = pl.multiple_of(block_start(route.peer(me, k), count, tokens), ROWS)
            att_ref[pl.ds(start, count), :] = pieces[0][k, 0] if route.whole else pieces[k][0]
        mid = x_ref[0, 0].astype(jnp.float32) + jnp.dot(
            att_ref[...], time_out_ref[...], preferred_element_type=jnp.float32
        )
        mid_ref[...] = mid.astype(jnp.bfloat16)
        normed = normalise(mid_ref[...].astype(jnp.float32), gain_ref[...])
        project_heads(normed, weight_ref, qkv_ref)
        bias = jnp.where(lax.broadcasted_iota(jnp.int32, (1, tokens), 1) < token_end, 0.0, NEG).astype(jnp.float32)
        attend(qkv_ref, pl.ds(0, tokens), bias, att_ref)
        result = mid_ref[...].astype(jnp.float32) + jnp.dot(
            att_ref[...], space_out_ref[...], preferred_element_type=jnp.float32
        )
        keep = lax.broadcasted_iota(jnp.int32, (tokens, 1), 0) < token_end
        out_ref[0, 0] = jnp.where(keep, result, 0.0).astype(jnp.bfloat16)

    @pl.when(jnp.logical_not(live))
    def _():
        out_ref[...] = jnp.zeros_like(out_ref)


def space_step(route, slot, counts, tokens, pieces, offset, first, calls, weights, partial):
    _, frames, places, width = tokens.shape
    devices, count = route.devices, route.count
    skip = first - offset
    unit = pl.BlockSpec((1, 1, places, width), lambda i, c, t: (clip_at(slot, c), first + i, 0, 0))
    if route.whole:
        piece_specs = [pl.BlockSpec((devices, 1, count, HW), lambda i, *_: (0, skip + i, 0, 0))]
    else:
        piece_specs = [pl.BlockSpec((1, count, HW), lambda i, *_: (skip + i, 0, 0))] * devices
    aliased = partial is not None
    operands = [*counts, tokens, *pieces, *weights] + ([partial] if aliased else [])
    return pl.pallas_call(
        functools.partial(space_kernel, route, frames, slot, first, int(aliased)),
        grid_spec=pltpu.PrefetchScalarGridSpec(
            num_scalar_prefetch=2,
            grid=(calls,),
            in_specs=[unit] + piece_specs + [KEPT(a) for a in weights] + ([ANY] if aliased else []),
            out_specs=unit,
            scratch_shapes=[
                pltpu.VMEM((places, HW), jnp.bfloat16),
                pltpu.VMEM((places, width), jnp.bfloat16),
                pltpu.VMEM((places, 3 * HW), jnp.bfloat16),
            ],
        ),
        out_shape=jax.ShapeDtypeStruct(tokens.shape, jnp.bfloat16),
        input_output_aliases={len(operands) - 1: 0} if aliased else {},
        compiler_params=pltpu.CompilerParams(vmem_limit_bytes=VMEM_LIMIT),
        cost_estimate=pl.CostEstimate(
            flops=4 * calls * places * width * 5 * HW, bytes_accessed=8_000_000, transcendentals=0
        ),
        name="space_block",
    )(*operands)


def pack_kernel(route, slot, counts, x_ref, *refs):
    outs = refs[:-3]
    held, in_sems, out_sems = refs[-3:]
    devices, count = route.devices, route.count
    first = 0 if route.whole else 1
    clip = clip_at(slot, counts)
    loads, stores = [], []
    for k in range(first, devices):
        start = pl.multiple_of(block_start(route.peer(lax.axis_index("frame"), k), count, x_ref.shape[2]), ROWS)
        loads.append(pltpu.make_async_copy(x_ref.at[clip, :, pl.ds(start, count), :], held.at[k], in_sems.at[k]))
        target = outs[0].at[k] if route.whole else outs[k - first]
        stores.append(pltpu.make_async_copy(held.at[k], target, out_sems.at[k]))
    for load in loads:
        load.start()
    for load, store in zip(loads, stores):
        load.wait()
        store.start()
    for store in stores:
        store.wait()


def pack_step(route, slot, frame_count, tokens):
    _, frames, _, width = tokens.shape
    devices, count = route.devices, route.count
    if route.whole:
        out_shape = [jax.ShapeDtypeStruct((devices, frames, count, width), jnp.bfloat16)]
    else:
        out_shape = [jax.ShapeDtypeStruct((frames, count, width), jnp.bfloat16)] * (devices - 1)
    return pl.pallas_call(
        functools.partial(pack_kernel, route, slot),
        in_specs=[pl.BlockSpec(memory_space=pltpu.SMEM), ANY],
        out_specs=[ANY] * len(out_shape),
        out_shape=out_shape,
        scratch_shapes=[
            pltpu.VMEM((devices, frames, count, width), jnp.bfloat16),
            pltpu.SemaphoreType.DMA((devices,)),
            pltpu.SemaphoreType.DMA((devices,)),
        ],
        compiler_params=pltpu.CompilerParams(vmem_limit_bytes=VMEM_LIMIT),
        name="pack_tokens",
    )(frame_count, tokens)


def exchange_all(block):
    return lax.all_to_all(block, "frame", 0, 0, tiled=True)


def exchange(block, devices, k):
    return lax.ppermute(block, "frame", [(i, i ^ k) for i in range(devices)])


def far_and_near(devices):
    half = devices // 2
    order = []
    for k in range(half):
        order += [half + k, k + 1]
    return order[: devices - 1]


def per_device(
    devices,
    video_tokens,
    frame_count,
    token_count,
    time_gain,
    time_qkv,
    time_out,
    space_gain,
    space_qkv,
    space_out,
):
    _, frames, places, _ = video_tokens.shape
    time_weights = (time_gain[None, :], time_qkv)
    space_weights = (space_gain[None, :], time_out, space_qkv, space_out)
    counts = (frame_count, token_count)
    half = frames // 2
    one = Route(True, devices, places // devices)
    two = Route(False, devices, places // devices)
    order = far_and_near(devices)

    (sent_a,) = pack_step(one, 0, frame_count, video_tokens)
    got_a = exchange_all(sent_a)
    sent_b = pack_step(two, 1, frame_count, video_tokens)
    got_b = {}
    for place, k in enumerate(order):
        if place == AHEAD:
            sent_b, got_a = lax.optimization_barrier((sent_b, got_a))
        got_b[k] = exchange(sent_b[k - 1], devices, k)
    (att_a,) = time_step(one, 0, frame_count, video_tokens, got_a, *time_weights)
    for k in order[: len(order) - BEHIND]:
        att_a, got_b[k] = lax.optimization_barrier((att_a, got_b[k]))
    back_a = exchange_all(att_a)
    received = [got_b[k] for k in range(1, devices)]
    *early_b, late_b = time_step(two, 1, frame_count, video_tokens, received, *time_weights, early=half)
    back_b = {k: exchange(early_b[k], devices, k) for k in order}
    late_b = exchange_all(late_b)
    back_b = [early_b[0]] + [back_b[k] for k in range(1, devices)]
    out = space_step(one, 0, counts, video_tokens, [back_a], 0, 0, frames, space_weights, None)
    out = space_step(two, 1, counts, video_tokens, back_b, 0, 0, half, space_weights, out)
    return space_step(one, 1, counts, video_tokens, [late_b], half, half, frames - half, space_weights, out)


def solution(mesh):
    placed = (P("clip", "frame", None, None), P("clip"), P("clip"), P(), P(), P(), P(), P(), P())
    return jax.shard_map(
        functools.partial(per_device, mesh.shape["frame"]),
        mesh=mesh,
        in_specs=placed,
        out_specs=P("clip", "frame", None, None),
        check_vma=False,
    )
```

time: 281 us -> 184 us (0.65)
  Pallas kernels: 174 us -> 66.6 us
  waiting for transfers between devices: 1.74 us -> 65.7 us
  starting transfers between devices: 96.3 us -> 40.1 us
  local copies, waits for them, and re-layouts: 6.09 us -> 11.2 us
    pallas_call x7, Pallas kernels: 174 us -> 66.6 us  [the longest x3 35.9 us: space_step(): pl.pallas_call(functools.partial(space_kernel, route, frames, slot, first...]
    ppermute x35 -> x14, starting transfers between devices: 96.3 us -> 22.3 us  [exchange(): return lax.ppermute(block, 'frame', [(i, i ^ k) for i in range(devices)])]
    all_to_all x0 -> x3, waiting for transfers between devices: none -> 45.4 us  [exchange_all(): return lax.all_to_all(block, 'frame', 0, 0, tiled=True)]
    ppermute x35 -> x14, waiting for transfers between devices: 1.74 us -> 20.3 us  [exchange(): return lax.ppermute(block, 'frame', [(i, i ^ k) for i in range(devices)])]
    all_to_all x0 -> x3, starting transfers between devices: none -> 17.7 us  [exchange_all(): return lax.all_to_all(block, 'frame', 0, 0, tiled=True)]
    unnamed x18 -> x46, local copies, waits for them, and re-layouts: 0.04 us -> 11.2 us
    another operation x3 -> x0, local copies, waits for them, and re-layouts: 3.98 us -> none  [space_info(): jnp.stack([jnp.int32(c), me, frame_count[c], token_count[c], first_frame,...]
  transfers between devices with their start and end apart: 35 -> 17, of which waited for: 2 -> 4; matrix products, arithmetic and copies ran while one was open for 2% -> 0% of each run, Pallas kernels for 38% -> 29%
where the time goes in v1:
time: 184 us
  Pallas kernels  66.6 us (36%)
  waiting for transfers between devices  65.7 us (36%)
  starting transfers between devices  40.1 us (22%)
  local copies, waits for them, and re-layouts  11.2 us (6%)
    all_to_all x3, waiting for transfers between devices, exchange_all(): return lax.all_to_all(block, 'frame', 0, 0, tiled=True)  45.4 us
    pallas_call x3, Pallas kernels, space_step(): pl.pallas_call(functools.partial(space_kernel, route, frames, slot, first...  35.9 us
    pallas_call x2, Pallas kernels, time_step(): pl.pallas_call(functools.partial(time_kernel, route, frames, slot), grid_...  25 us
    ppermute x14, starting transfers between devices, exchange(): return lax.ppermute(block, 'frame', [(i, i ^ k) for i in range(devices)])  22.3 us
    ppermute x14, waiting for transfers between devices, exchange(): return lax.ppermute(block, 'frame', [(i, i ^ k) for i in range(devices)])  20.3 us
    all_to_all x3, starting transfers between devices, exchange_all(): return lax.all_to_all(block, 'frame', 0, 0, tiled=True)  17.7 us
    unnamed x46, local copies, waits for them, and re-layouts  11.2 us
    pallas_call x2, Pallas kernels, pack_step(): pl.pallas_call(functools.partial(pack_kernel, route, slot), in_specs=[pl....  5.65 us
  transfers between devices with their start and end apart: 17, of which 4 were waited for; matrix products, arithmetic and copies ran while one was open for 0% of the time, Pallas kernels for 29%

profile of v1, /device:TPU:0, one launch (start us, length us, event | category | flops | bytes accessed | tf_op | source)
XLA Modules:
  0.0 183.8 jit_solution(14595464213952876860)
XLA Ops:
  0.7 2.9 %pack_tokens.3 = bf16[8,4,32,1024]{3,2,1,0:T(8,128)(2,1)} custom-call(s32[2]{0:T(128)S(1)} %copy-done, bf16[2,4,256,1024]{3,2,1,0:T(8,128)(2,1)} %x_ref.9), custom_call_target="tpu_custom_call" | custom-call | tf_op jit(solution)/shard_map/pack_tokens/pallas_call | solution.py:265
  3.6 7.3 %all-to-all-start = ((bf16[8,4,32,1024]{3,2,1,0:T(8,128)(2,1)}), bf16[8,4,32,1024]{3,2,1,0:T(8,128)(2,1)S(1)}, u32[]{:S(2)}, u32[]{:S(2)}) async-start(bf16[8,4,32,1024]{3,2,1,0:T(8,128)(2,1)} %pack_tokens.3), calls=%async_computation | async-start | bytes 4194304 | tf_op jit(solution)/shard_map/all_to_all | solution.py:281
  10.9 2.7 %pack_tokens.2 = (bf16[4,32,1024]{2,1,0:T(8,128)(2,1)}, bf16[4,32,1024]{2,1,0:T(8,128)(2,1)S(1)}, bf16[4,32,1024]{2,1,0:T(8,128)(2,1)S(1)}, bf16[4,32,1024]{2,1,...) custom-call(s32[2]{0:T(128)S(1)} %copy-done.1, ...), custom_call_target="tpu_custom_call" | custom-call | tf_op jit(solution)/shard_map/pack_tokens/pallas_call | solution.py:265
  15.1 44.1 %all-to-all-done.refs_0_ = bf16[8,4,32,1024]{3,2,1,0:T(8,128)(2,1)S(1)} async-done(((bf16[8,4,32,1024]{3,2,1,0:T(8,128)(2,1)}), bf16[8,4,32,1024]{3,2,1,0:T(8,128)(2,1)S(1)}, u32[]{:S(2)}, u32[]{:S(2)}) %all-to-all-start) | async-done | bytes 2097184 | tf_op jit(solution)/shard_map/all_to_all | solution.py:281
  59.2 1.5 collective-permute-start.1
  60.6 2.9 %collective-permute-start.2 = (bf16[4,32,1024]{2,1,0:T(8,128)(2,1)}, bf16[4,32,1024]{2,1,0:T(8,128)(2,1)S(1)}, u32[]{:S(2)}, u32[]{:S(2)}) collective-permute-start(bf16[4,32,1024]{2,1,0:T(8,128)(2,1)} %get-tuple-element.56), channel_id=1, source_target_pairs={{0,5},{1,4},{2,7},{3,6},{4,1},{5,0},{6,3},{7,2},{8,13},{9,12},{10,... | collective-permute-start | bytes 786440 | tf_op jit(solution)/shard_map/ppermute | solution.py:285
  63.5 2.3 %collective-permute-start.4 = (bf16[4,32,1024]{2,1,0:T(8,128)(2,1)}, bf16[4,32,1024]{2,1,0:T(8,128)(2,1)S(1)}, u32[]{:S(2)}, u32[]{:S(2)}) collective-permute-start(bf16[4,32,1024]{2,1,0:T(8,128)(2,1)} %copy-done.14), channel_id=1, source_target_pairs={{0,6},{1,7},{2,4},{3,5},{4,2},{5,3},{6,0},{7,1},{8,14},{9,15},{10,... | collective-permute-start | bytes 786440 | tf_op jit(solution)/shard_map/ppermute | solution.py:285
  65.8 14.3 %collective-permute-done.refs_4_ = bf16[4,32,1024]{2,1,0:T(8,128)(2,1)S(1)} collective-permute-done((bf16[4,32,1024]{2,1,0:T(8,128)(2,1)}, bf16[4,32,1024]{2,1,0:T(8,128)(2,1)S(1)}, u32[]{:S(2)}, u32[]{:S(2)}) %collective-permute-start) | collective-permute-done | bytes 262176 | tf_op jit(solution)/shard_map/ppermute | solution.py:285
  80.2 2.5 %collective-permute-start.6 = (bf16[4,32,1024]{2,1,0:T(8,128)(2,1)S(1)}, bf16[4,32,1024]{2,1,0:T(8,128)(2,1)S(1)}, u32[]{:S(2)}, u32[]{:S(2)}) collective-permute-start(bf16[4,32,1024]{2,1,0:T(8,128)(2,1)S(1)} %get-tuple-element.69), channel_id=1, source_target_pairs={{0,7},{1,6},{2,5},{3,4},{4,3},{5,2},{6,1},{7,0},{8,15},{9,14},{10,... | collective-permute-start | bytes 786440 | tf_op jit(solution)/shard_map/ppermute | solution.py:285
  82.7 12.4 %time_attention.2 = bf16[8,4,32,512]{3,2,1,0:T(8,128)(2,1)} custom-call(s32[2]{0:T(128)S(1)} %copy-done.1, bf16[8,4,32,1024]{3,2,1,0:T(8,128)(2,1)S(1)} %all-to-all-done.refs_0_, f32[1,1024]{1,0:T(1,128)S(1)} %bitcast.2, bf16[1024,1536]{1,0:T(8,128)(2,1)} %refs_9_.2), custom_call_target="tpu_custom_call" | custom-call | flops 6442450944 | bytes 12000000 | tf_op jit(solution)/shard_map/time_attention/pallas_call | solution.py:144
  95.2 0.8 copy-done.12
  95.9 6.0 %collective-permute-done.5.refs_3_ = bf16[4,32,1024]{2,1,0:T(8,128)(2,1)S(1)} collective-permute-done((bf16[4,32,1024]{2,1,0:T(8,128)(2,1)S(1)}, bf16[4,32,1024]{2,1,0:T(8,128)(2,1)S(1)}, u32[]{:S(2)}, u32[]{:S(2)}) %collective-permute-start.5) | collective-permute-done | bytes 262176 | tf_op jit(solution)/shard_map/ppermute | solution.py:285
  103.4 6.8 %all-to-all-start.2 = ((bf16[8,4,32,512]{3,2,1,0:T(8,128)(2,1)}), bf16[8,4,32,512]{3,2,1,0:T(8,128)(2,1)S(1)}, u32[]{:S(2)}, u32[]{:S(2)}) async-start(bf16[8,4,32,512]{3,2,1,0:T(8,128)(2,1)} %time_attention.2), calls=%async_computation.2 | async-start | bytes 2097152 | tf_op jit(solution)/shard_map/all_to_all | solution.py:281
  110.2 0.9 copy-done.7
  111.1 0.9 copy-done.9
  112.1 0.9 copy-done.11
  113.0 0.9 copy-done.13
  114.0 0.9 copy-done.17
  114.9 0.9 copy-done.19
  115.9 12.6 %time_attention.3 = (bf16[2,32,512]{2,1,0:T(8,128)(2,1)S(1)}, bf16[2,32,512]{2,1,0:T(8,128)(2,1)S(1)}, bf16[2,32,512]{2,1,0:T(8,128)(2,1)S(1)}, bf16[2,32,512]{2...) custom-call(s32[2]{0:T(128)S(1)} %copy-done.1, ...), custom_call_target="tpu_custom_call" | custom-call | flops 6442450944 | bytes 12000000 | tf_op jit(solution)/shard_map/time_attention/pallas_call | solution.py:144
  128.4 2.0 %collective-permute-start.7 = (bf16[2,32,512]{2,1,0:T(8,128)(2,1)S(1)}, bf16[2,32,512]{2,1,0:T(8,128)(2,1)S(1)}, u32[]{:S(2)}, u32[]{:S(2)}) collective-permute-start(bf16[2,32,512]{2,1,0:T(8,128)(2,1)S(1)} %get-tuple-element.73), channel_id=1, source_target_pairs={{0,1},{1,0},{2,3},{3,2},{4,5},{5,4},{6,7},{7,6},{8,9},{9,8},{10,11... | collective-permute-start | bytes 196616 | tf_op jit(solution)/shard_map/ppermute | solution.py:285
  130.5 1.5 collective-permute-start.8
  132.1 2.7 %collective-permute-start.10 = (bf16[2,32,512]{2,1,0:T(8,128)(2,1)S(1)}, bf16[2,32,512]{2,1,0:T(8,128)(2,1)S(1)}, u32[]{:S(2)}, u32[]{:S(2)}) collective-permute-start(bf16[2,32,512]{2,1,0:T(8,128)(2,1)S(1)} %get-tuple-element.76), channel_id=1, source_target_pairs={{0,4},{1,5},{2,6},{3,7},{4,0},{5,1},{6,2},{7,3},{8,12},{9,13},{10,... | collective-permute-start | bytes 196616 | tf_op jit(solution)/shard_map/ppermute | solution.py:285
  134.8 1.5 collective-permute-start.11
  136.3 1.3 all-to-all-done.2.refs_0_
  137.6 3.7 %all-to-all-start.1 = ((bf16[8,2,32,512]{3,2,1,0:T(8,128)(2,1)}), bf16[8,2,32,512]{3,2,1,0:T(8,128)(2,1)S(1)}, u32[]{:S(2)}, u32[]{:S(2)}) async-start(bf16[8,2,32,512]{3,2,1,0:T(8,128)(2,1)} %get-tuple-element.71), calls=%async_computation.1 | async-start | bytes 1048576 | tf_op jit(solution)/shard_map/all_to_all | solution.py:281
  141.3 3.6 %collective-permute-start.12 = (bf16[2,32,512]{2,1,0:T(8,128)(2,1)S(1)}, bf16[2,32,512]{2,1,0:T(8,128)(2,1)S(1)}, u32[]{:S(2)}, u32[]{:S(2)}) collective-permute-start(bf16[2,32,512]{2,1,0:T(8,128)(2,1)S(1)} %get-tuple-element.78), channel_id=1, source_target_pairs={{0,6},{1,7},{2,4},{3,5},{4,2},{5,3},{6,0},{7,1},{8,14},{9,15},{10,... | collective-permute-start | bytes 196616 | tf_op jit(solution)/shard_map/ppermute | solution.py:285
  144.8 1.7 collective-permute-start.13
  146.5 1.2 copy-done.3
  147.8 16.3 %space_block.3.refs_12_ = bf16[2,4,256,1024]{3,2,1,0:T(8,128)(2,1)} custom-call(s32[2]{0:T(128)S(1)} %copy-done.1, s32[2]{0:T(128)S(1)} %copy-done.22, bf16[2,4,256,1024]{3,2,1,0:T(8,128)(2,1)} %x_ref.9, bf16[8,4,32,512]{3,2,1,0:T(8,128)(2,1)S(1)} %all-to-all-done.2.refs_0_, f32[1,1024]{1,0:T(1,128)S(1)} %bitcast.4, bf16[512,1024]{1,0:T(8,128)(2,1)S(1)} %copy-done.2, ...), custom_call_target="tpu_custom_call" | custom-call | flops 10737418240 | bytes 8000000 | tf_op jit(solution)/shard_map/space_block/pallas_call | solution.py:214
  164.1 9.8 %space_block.4.refs_5_ = bf16[2,4,256,1024]{3,2,1,0:T(8,128)(2,1)} custom-call(s32[2]{0:T(128)S(1)} %copy-done.1, s32[2]{0:T(128)S(1)} %copy-done.22, bf16[2,4,256,1024]{3,2,1,0:T(8,128)(2,1)} %x_ref.9, bf16[2,32,512]{2,1,0:T(8,128)(2,1)S(1)} %get-tuple-element.72.refs_0_, ...), custom_call_target="tpu_custom_call", output_to_operand_aliasing={{}: (15, {})} | custom-call | flops 5368709120 | bytes 8000000 | tf_op jit(solution)/shard_map/space_block/pallas_call | solution.py:214
  173.9 9.8 %space_block.5 = bf16[2,4,256,1024]{3,2,1,0:T(8,128)(2,1)} custom-call(s32[2]{0:T(128)S(1)} %copy-done.1, s32[2]{0:T(128)S(1)} %copy-done.22, bf16[2,4,256,1024]{3,2,1,0:T(8,128)(2,1)} %x_ref.9, bf16[8,2,32,512]{3,2,1,0:T(8,128)(2,1)S(1)} %all-to-all-done.1.refs_0_, f32[1,1024]{1,0:T(1,128)S(1)} %bitcast.6, ...), custom_call_target="tpu_custom_call", output_to_operand_aliasing={{}: (8, {})} | custom-call | flops 5368709120 | bytes 8000000 | tf_op jit(solution)/shard_map/space_block/pallas_call | solution.py:214
  (55 shorter events, 3.8 us)
Async XLA Ops:
  0.7 10.3 %copy-start.1 = (s32[2]{0:T(128)S(1)}, s32[2]{0:T(128)}, u32[]{:S(2)}) copy-start(s32[2]{0:T(128)} %frame_count.9) | copy-start | bytes 28
  3.6 79.1 %copy-start.20 = (f32[1024]{0:T(1024)S(1)}, f32[1024]{0:T(1024)}, u32[]{:S(2)}) copy-start(f32[1024]{0:T(1024)} %param.12) | copy-start | bytes 12292
  3.6 55.5 %all-to-all-start = ((bf16[8,4,32,1024]{3,2,1,0:T(8,128)(2,1)}), bf16[8,4,32,1024]{3,2,1,0:T(8,128)(2,1)S(1)}, u32[]{:S(2)}, u32[]{:S(2)}) async-start(bf16[8,4,32,1024]{3,2,1,0:T(8,128)(2,1)} %pack_tokens.3), calls=%async_computation | async-start | bytes 4194304 | tf_op jit(solution)/shard_map/all_to_all | solution.py:281
  59.1 21.0 %collective-permute-start = (bf16[4,32,1024]{2,1,0:T(8,128)(2,1)}, bf16[4,32,1024]{2,1,0:T(8,128)(2,1)S(1)}, u32[]{:S(2)}, u32[]{:S(2)}) collective-permute-start(bf16[4,32,1024]{2,1,0:T(8,128)(2,1)} %get-tuple-element.51), channel_id=1, source_target_pairs={{0,4},{1,5},{2,6},{3,7},{4,0},{5,1},{6,2},{7,3},{8,12},{9,13},{10,... | collective-permute-start | bytes 786440 | tf_op jit(solution)/shard_map/ppermute | solution.py:285
  59.2 21.0 %collective-permute-start.1 = (bf16[4,32,1024]{2,1,0:T(8,128)(2,1)}, bf16[4,32,1024]{2,1,0:T(8,128)(2,1)S(1)}, u32[]{:S(2)}, u32[]{:S(2)}) collective-permute-start(bf16[4,32,1024]{2,1,0:T(8,128)(2,1)} %get-tuple-element.53), channel_id=1, source_target_pairs={{0,1},{1,0},{2,3},{3,2},{4,5},{5,4},{6,7},{7,6},{8,9},{9,8},{10,11... | collective-permute-start | bytes 786440 | tf_op jit(solution)/shard_map/ppermute | solution.py:285
  60.6 34.5 %collective-permute-start.2 = (bf16[4,32,1024]{2,1,0:T(8,128)(2,1)}, bf16[4,32,1024]{2,1,0:T(8,128)(2,1)S(1)}, u32[]{:S(2)}, u32[]{:S(2)}) collective-permute-start(bf16[4,32,1024]{2,1,0:T(8,128)(2,1)} %get-tuple-element.56), channel_id=1, source_target_pairs={{0,5},{1,4},{2,7},{3,6},{4,1},{5,0},{6,3},{7,2},{8,13},{9,12},{10,... | collective-permute-start | bytes 786440 | tf_op jit(solution)/shard_map/ppermute | solution.py:285
  63.5 31.6 %collective-permute-start.3 = (bf16[4,32,1024]{2,1,0:T(8,128)(2,1)}, bf16[4,32,1024]{2,1,0:T(8,128)(2,1)S(1)}, u32[]{:S(2)}, u32[]{:S(2)}) collective-permute-start(bf16[4,32,1024]{2,1,0:T(8,128)(2,1)} %copy-done.15), channel_id=1, source_target_pairs={{0,2},{1,3},{2,0},{3,1},{4,6},{5,7},{6,4},{7,5},{8,10},{9,11},{10,... | collective-permute-start | bytes 786440 | tf_op jit(solution)/shard_map/ppermute | solution.py:285
  63.5 31.6 %collective-permute-start.4 = (bf16[4,32,1024]{2,1,0:T(8,128)(2,1)}, bf16[4,32,1024]{2,1,0:T(8,128)(2,1)S(1)}, u32[]{:S(2)}, u32[]{:S(2)}) collective-permute-start(bf16[4,32,1024]{2,1,0:T(8,128)(2,1)} %copy-done.14), channel_id=1, source_target_pairs={{0,6},{1,7},{2,4},{3,5},{4,2},{5,3},{6,0},{7,1},{8,14},{9,15},{10,... | collective-permute-start | bytes 786440 | tf_op jit(solution)/shard_map/ppermute | solution.py:285
  80.1 21.8 %collective-permute-start.5 = (bf16[4,32,1024]{2,1,0:T(8,128)(2,1)S(1)}, bf16[4,32,1024]{2,1,0:T(8,128)(2,1)S(1)}, u32[]{:S(2)}, u32[]{:S(2)}) collective-permute-start(bf16[4,32,1024]{2,1,0:T(8,128)(2,1)S(1)} %get-tuple-element.63), channel_id=1, source_target_pairs={{0,3},{1,2},{2,1},{3,0},{4,7},{5,6},{6,5},{7,4},{8,11},{9,10},{10,... | collective-permute-start | bytes 786440 | tf_op jit(solution)/shard_map/ppermute | solution.py:285
  80.2 15.0 %copy-start.6 = (bf16[4,32,1024]{2,1,0:T(8,128)(2,1)}, bf16[4,32,1024]{2,1,0:T(8,128)(2,1)S(1)}, u32[]{:S(2)}) copy-start(bf16[4,32,1024]{2,1,0:T(8,128)(2,1)S(1)} %collective-permute-done.1.refs_1_) | copy-start | bytes 786436
  80.2 22.5 %collective-permute-start.6 = (bf16[4,32,1024]{2,1,0:T(8,128)(2,1)S(1)}, bf16[4,32,1024]{2,1,0:T(8,128)(2,1)S(1)}, u32[]{:S(2)}, u32[]{:S(2)}) collective-permute-start(bf16[4,32,1024]{2,1,0:T(8,128)(2,1)S(1)} %get-tuple-element.69), channel_id=1, source_target_pairs={{0,7},{1,6},{2,5},{3,4},{4,3},{5,2},{6,1},{7,0},{8,15},{9,14},{10,... | collective-permute-start | bytes 786440 | tf_op jit(solution)/shard_map/ppermute | solution.py:285
  95.1 8.2 %copy-start.8 = (bf16[4,32,1024]{2,1,0:T(8,128)(2,1)}, bf16[4,32,1024]{2,1,0:T(8,128)(2,1)S(1)}, u32[]{:S(2)}) copy-start(bf16[4,32,1024]{2,1,0:T(8,128)(2,1)S(1)} %collective-permute-done.2.refs_5_) | copy-start | bytes 786436
  95.1 8.2 %copy-start.10 = (bf16[4,32,1024]{2,1,0:T(8,128)(2,1)}, bf16[4,32,1024]{2,1,0:T(8,128)(2,1)S(1)}, u32[]{:S(2)}) copy-start(bf16[4,32,1024]{2,1,0:T(8,128)(2,1)S(1)} %collective-permute-done.3.refs_2_) | copy-start | bytes 786436
  103.4 34.2 %all-to-all-start.2 = ((bf16[8,4,32,512]{3,2,1,0:T(8,128)(2,1)}), bf16[8,4,32,512]{3,2,1,0:T(8,128)(2,1)S(1)}, u32[]{:S(2)}, u32[]{:S(2)}) async-start(bf16[8,4,32,512]{3,2,1,0:T(8,128)(2,1)} %time_attention.2), calls=%async_computation.2 | async-start | bytes 2097152 | tf_op jit(solution)/shard_map/all_to_all | solution.py:281
  110.2 0.9 copy-start.7
  111.1 0.9 copy-start.9
  112.1 0.9 copy-start.11
  113.0 0.9 copy-start.13
  115.9 30.7 %copy-start.2 = (bf16[512,1024]{1,0:T(8,128)(2,1)S(1)}, bf16[512,1024]{1,0:T(8,128)(2,1)}, u32[]{:S(2)}) copy-start(bf16[512,1024]{1,0:T(8,128)(2,1)} %refs_2_.5) | copy-start | bytes 3145732
  115.9 30.7 %copy-start.21 = (f32[1024]{0:T(1024)S(1)}, f32[1024]{0:T(1024)}, u32[]{:S(2)}) copy-start(f32[1024]{0:T(1024)} %param.15) | copy-start | bytes 12292
  115.9 30.7 %copy-start.22 = (s32[2]{0:T(128)S(1)}, s32[2]{0:T(128)}, u32[]{:S(2)}) copy-start(s32[2]{0:T(128)} %token_count.5) | copy-start | bytes 28
  128.4 12.8 %collective-permute-start.7 = (bf16[2,32,512]{2,1,0:T(8,128)(2,1)S(1)}, bf16[2,32,512]{2,1,0:T(8,128)(2,1)S(1)}, u32[]{:S(2)}, u32[]{:S(2)}) collective-permute-start(bf16[2,32,512]{2,1,0:T(8,128)(2,1)S(1)} %get-tuple-element.73), channel_id=1, source_target_pairs={{0,1},{1,0},{2,3},{3,2},{4,5},{5,4},{6,7},{7,6},{8,9},{9,8},{10,11... | collective-permute-start | bytes 196616 | tf_op jit(solution)/shard_map/ppermute | solution.py:285
  130.5 14.4 %collective-permute-start.8 = (bf16[2,32,512]{2,1,0:T(8,128)(2,1)S(1)}, bf16[2,32,512]{2,1,0:T(8,128)(2,1)S(1)}, u32[]{:S(2)}, u32[]{:S(2)}) collective-permute-start(bf16[2,32,512]{2,1,0:T(8,128)(2,1)S(1)} %get-tuple-element.74), channel_id=1, source_target_pairs={{0,2},{1,3},{2,0},{3,1},{4,6},{5,7},{6,4},{7,5},{8,10},{9,11},{10,... | collective-permute-start | bytes 196616 | tf_op jit(solution)/shard_map/ppermute | solution.py:285
  131.9 32.1 %collective-permute-start.9 = (bf16[2,32,512]{2,1,0:T(8,128)(2,1)S(1)}, bf16[2,32,512]{2,1,0:T(8,128)(2,1)S(1)}, u32[]{:S(2)}, u32[]{:S(2)}) collective-permute-start(bf16[2,32,512]{2,1,0:T(8,128)(2,1)S(1)} %get-tuple-element.75), channel_id=1, source_target_pairs={{0,3},{1,2},{2,1},{3,0},{4,7},{5,6},{6,5},{7,4},{8,11},{9,10},{10,... | collective-permute-start | bytes 196616 | tf_op jit(solution)/shard_map/ppermute | solution.py:285
  132.1 31.9 %collective-permute-start.10 = (bf16[2,32,512]{2,1,0:T(8,128)(2,1)S(1)}, bf16[2,32,512]{2,1,0:T(8,128)(2,1)S(1)}, u32[]{:S(2)}, u32[]{:S(2)}) collective-permute-start(bf16[2,32,512]{2,1,0:T(8,128)(2,1)S(1)} %get-tuple-element.76), channel_id=1, source_target_pairs={{0,4},{1,5},{2,6},{3,7},{4,0},{5,1},{6,2},{7,3},{8,12},{9,13},{10,... | collective-permute-start | bytes 196616 | tf_op jit(solution)/shard_map/ppermute | solution.py:285
  134.8 29.2 %collective-permute-start.11 = (bf16[2,32,512]{2,1,0:T(8,128)(2,1)S(1)}, bf16[2,32,512]{2,1,0:T(8,128)(2,1)S(1)}, u32[]{:S(2)}, u32[]{:S(2)}) collective-permute-start(bf16[2,32,512]{2,1,0:T(8,128)(2,1)S(1)} %get-tuple-element.77), channel_id=1, source_target_pairs={{0,5},{1,4},{2,7},{3,6},{4,1},{5,0},{6,3},{7,2},{8,13},{9,12},{10,... | collective-permute-start | bytes 196616 | tf_op jit(solution)/shard_map/ppermute | solution.py:285
  137.6 36.4 %all-to-all-start.1 = ((bf16[8,2,32,512]{3,2,1,0:T(8,128)(2,1)}), bf16[8,2,32,512]{3,2,1,0:T(8,128)(2,1)S(1)}, u32[]{:S(2)}, u32[]{:S(2)}) async-start(bf16[8,2,32,512]{3,2,1,0:T(8,128)(2,1)} %get-tuple-element.71), calls=%async_computation.1 | async-start | bytes 1048576 | tf_op jit(solution)/shard_map/all_to_all | solution.py:281
  141.3 22.8 %collective-permute-start.12 = (bf16[2,32,512]{2,1,0:T(8,128)(2,1)S(1)}, bf16[2,32,512]{2,1,0:T(8,128)(2,1)S(1)}, u32[]{:S(2)}, u32[]{:S(2)}) collective-permute-start(bf16[2,32,512]{2,1,0:T(8,128)(2,1)S(1)} %get-tuple-element.78), channel_id=1, source_target_pairs={{0,6},{1,7},{2,4},{3,5},{4,2},{5,3},{6,0},{7,1},{8,14},{9,15},{10,... | collective-permute-start | bytes 196616 | tf_op jit(solution)/shard_map/ppermute | solution.py:285
  144.8 19.2 %collective-permute-start.13 = (bf16[2,32,512]{2,1,0:T(8,128)(2,1)S(1)}, bf16[2,32,512]{2,1,0:T(8,128)(2,1)S(1)}, u32[]{:S(2)}, u32[]{:S(2)}) collective-permute-start(bf16[2,32,512]{2,1,0:T(8,128)(2,1)S(1)} %get-tuple-element.79), channel_id=1, source_target_pairs={{0,7},{1,6},{2,5},{3,4},{4,3},{5,2},{6,1},{7,0},{8,15},{9,14},{10,... | collective-permute-start | bytes 196616 | tf_op jit(solution)/shard_map/ppermute | solution.py:285
  146.5 1.2 copy-start.3
  147.8 16.3 %copy-start.4 = (bf16[512,1024]{1,0:T(8,128)(2,1)S(1)}, bf16[512,1024]{1,0:T(8,128)(2,1)}, u32[]{:S(2)}) copy-start(bf16[512,1024]{1,0:T(8,128)(2,1)} %refs_4_.3) | copy-start | bytes 3145732
  164.1 9.8 %copy-start.5 = (bf16[512,1024]{1,0:T(8,128)(2,1)S(1)}, bf16[512,1024]{1,0:T(8,128)(2,1)}, u32[]{:S(2)}) copy-start(bf16[512,1024]{1,0:T(8,128)(2,1)} %refs_4_.3) | copy-start | bytes 3145732
  (8 other events, 6.2 us)

commit v2 on v1

--- a/solution.py
+++ b/solution.py
@@ -12,9 +12,9 @@
 HW = 512
 ROWS = 16
 NEG = -1e30
-AHEAD = 0
-BEHIND = 0
-VMEM_LIMIT = 50 * 1024 * 1024
+LEAD = 2
+TAIL = 7
+VMEM_LIMIT = 56 * 1024 * 1024
 def KEPT(a):
     return pl.BlockSpec(a.shape, lambda i, *_: (0,) * a.ndim)
 
@@ -71,7 +71,7 @@
         return k if self.whole else me ^ k
 
 
-def time_kernel(route, frames, slot, frame_count, *refs):
+def time_kernel(route, back, frames, slot, frame_count, *refs):
     devices = route.devices
     n_in = 1 if route.whole else devices
     sources = refs[:n_in]
@@ -86,14 +86,14 @@
     def _():
         row = lax.broadcasted_iota(jnp.int32, (half, half), 0)
         col = lax.broadcasted_iota(jnp.int32, (half, half), 1)
-        frame = route.peer(me, col // group) * frames + (col // 8) % frames
+        frame = (back if route.whole else route).peer(me, col // group) * frames + (col // 8) % frames
         valid = (row % 8 == col % 8) & (frame < frame_count[clip_at(slot, frame_count)])
         bias_ref[...] = jnp.where(valid, 0.0, NEG).astype(jnp.float32)
 
     gain = gain_ref[...]
     for k in range(devices):
         if route.whole:
-            values = sources[0][k]
+            values = sources[0][back.peer(me, k)]
         else:
             values = sources[0][0] if k == 0 else sources[k][...]
         normed = values.astype(jnp.float32)
@@ -109,15 +109,13 @@
             for s in range(ROWS // 8)
         ]
         result = jnp.concatenate(pieces, axis=1).astype(jnp.bfloat16)
-        if route.whole:
-            outs[0][k] = result
+        if back.whole:
+            outs[0][route.peer(me, k)] = result
         else:
-            early = outs[k].shape[0]
-            outs[k][...] = result[:early]
-            outs[-1][route.peer(me, k)] = result[early:]
-
-
-def time_step(route, slot, frame_count, tokens, received, gain, weight, early=0):
+            outs[k][...] = result
+
+
+def time_step(route, back, slot, frame_count, tokens, received, gain, weight):
     _, frames, places, width = tokens.shape
     devices, count = route.devices, route.count
     rows = devices * frames * ROWS
@@ -130,19 +128,18 @@
     if route.whole:
         operands = [received]
         in_specs = [pl.BlockSpec((devices, frames, ROWS, width), lambda i, *_: (0, 0, i, 0))]
-        out_specs = [pl.BlockSpec((devices, frames, ROWS, HW), lambda i, *_: (0, 0, i, 0))]
-        out_shape = [jax.ShapeDtypeStruct((devices, frames, count, HW), jnp.bfloat16)]
     else:
         operands = [tokens, *received]
         in_specs = [pl.BlockSpec((1, frames, ROWS, width), own_block)]
         in_specs += [pl.BlockSpec((frames, ROWS, width), lambda i, *_: (0, i, 0))] * (devices - 1)
-        late = frames - early
-        out_specs = [pl.BlockSpec((early, ROWS, HW), lambda i, *_: (0, i, 0))] * devices
-        out_specs += [pl.BlockSpec((devices, late, ROWS, HW), lambda i, *_: (0, 0, i, 0))]
-        out_shape = [jax.ShapeDtypeStruct((early, count, HW), jnp.bfloat16)] * devices
-        out_shape += [jax.ShapeDtypeStruct((devices, late, count, HW), jnp.bfloat16)]
+    if back.whole:
+        out_specs = [pl.BlockSpec((devices, frames, ROWS, HW), lambda i, *_: (0, 0, i, 0))]
+        out_shape = [jax.ShapeDtypeStruct((devices, frames, count, HW), jnp.bfloat16)]
+    else:
+        out_specs = [pl.BlockSpec((frames, ROWS, HW), lambda i, *_: (0, i, 0))] * devices
+        out_shape = [jax.ShapeDtypeStruct((frames, count, HW), jnp.bfloat16)] * devices
     return pl.pallas_call(
-        functools.partial(time_kernel, route, frames, slot),
+        functools.partial(time_kernel, route, back, frames, slot),
         grid_spec=pltpu.PrefetchScalarGridSpec(
             num_scalar_prefetch=1,
             grid=(count // ROWS,),
@@ -309,7 +306,6 @@
     time_weights = (time_gain[None, :], time_qkv)
     space_weights = (space_gain[None, :], time_out, space_qkv, space_out)
     counts = (frame_count, token_count)
-    half = frames // 2
     one = Route(True, devices, places // devices)
     two = Route(False, devices, places // devices)
     order = far_and_near(devices)
@@ -317,23 +313,22 @@
     (sent_a,) = pack_step(one, 0, frame_count, video_tokens)
     got_a = exchange_all(sent_a)
     sent_b = pack_step(two, 1, frame_count, video_tokens)
-    got_b = {}
+    sent_b, _ = lax.optimization_barrier((sent_b, got_a))
+    got_b = {k: exchange(sent_b[k - 1], devices, k) for k in order}
+    att_a = time_step(one, two, 0, frame_count, video_tokens, got_a, *time_weights)
+    earlier = [got_b[k] for k in order]
+    back_a = {}
     for place, k in enumerate(order):
-        if place == AHEAD:
-            sent_b, got_a = lax.optimization_barrier((sent_b, got_a))
-        got_b[k] = exchange(sent_b[k - 1], devices, k)
-    (att_a,) = time_step(one, 0, frame_count, video_tokens, got_a, *time_weights)
-    for k in order[: len(order) - BEHIND]:
-        att_a, got_b[k] = lax.optimization_barrier((att_a, got_b[k]))
-    back_a = exchange_all(att_a)
+        block, _ = lax.optimization_barrier((att_a[k], earlier[: place + LEAD]))
+        back_a[k] = exchange(block, devices, k)
+        earlier.append(back_a[k])
     received = [got_b[k] for k in range(1, devices)]
-    *early_b, late_b = time_step(two, 1, frame_count, video_tokens, received, *time_weights, early=half)
-    back_b = {k: exchange(early_b[k], devices, k) for k in order}
-    late_b = exchange_all(late_b)
-    back_b = [early_b[0]] + [back_b[k] for k in range(1, devices)]
-    out = space_step(one, 0, counts, video_tokens, [back_a], 0, 0, frames, space_weights, None)
-    out = space_step(two, 1, counts, video_tokens, back_b, 0, 0, half, space_weights, out)
-    return space_step(one, 1, counts, video_tokens, [late_b], half, half, frames - half, space_weights, out)
+    (att_b,) = time_step(two, one, 1, frame_count, video_tokens, received, *time_weights)
+    att_b, _ = lax.optimization_barrier((att_b, earlier[: len(order) + TAIL]))
+    back_b = exchange_all(att_b)
+    back_a = [att_a[0]] + [back_a[k] for k in range(1, devices)]
+    out = space_step(two, 0, counts, video_tokens, back_a, 0, 0, frames, space_weights, None)
+    return space_step(one, 1, counts, video_tokens, [back_b], 0, 0, frames, space_weights, out)
 
 
 def solution(mesh):

time: 184 us -> 179 us (0.973)
  local copies, waits for them, and re-layouts: 11.2 us -> 1.04 us
  starting transfers between devices: 40.1 us -> 44.1 us
    unnamed x46 -> x32, local copies, waits for them, and re-layouts: 11.2 us -> 1.04 us
    ppermute x14, starting transfers between devices: 22.3 us -> 31.9 us  [exchange(): return lax.ppermute(block, 'frame', [(i, i ^ k) for i in range(devices)])]
    all_to_all x3 -> x2, waiting for transfers between devices: 45.4 us -> 52.3 us  [exchange_all(): return lax.all_to_all(block, 'frame', 0, 0, tiled=True)]
    all_to_all x3 -> x2, starting transfers between devices: 17.7 us -> 12.2 us  [exchange_all(): return lax.all_to_all(block, 'frame', 0, 0, tiled=True)]
    ppermute x14, waiting for transfers between devices: 20.3 us -> 15.2 us  [exchange(): return lax.ppermute(block, 'frame', [(i, i ^ k) for i in range(devices)])]
    pallas_call x3 -> x2, Pallas kernels: 35.9 us -> 34.3 us  [space_step(): pl.pallas_call(functools.partial(space_kernel, route, frames, slot, first...]
  transfers between devices with their start and end apart: 17 -> 16, of which waited for: 4 -> 5; matrix products, arithmetic and copies ran while one was open for 0% -> 0% of each run, Pallas kernels for 29% -> 26%
where the time goes in v2:
time: 179 us
  waiting for transfers between devices  67.5 us (38%)
  Pallas kernels  66.1 us (37%)
  starting transfers between devices  44.1 us (25%)
    all_to_all x2, waiting for transfers between devices, exchange_all(): return lax.all_to_all(block, 'frame', 0, 0, tiled=True)  52.3 us
    pallas_call x2, Pallas kernels, space_step(): pl.pallas_call(functools.partial(space_kernel, route, frames, slot, first...  34.3 us
    ppermute x14, starting transfers between devices, exchange(): return lax.ppermute(block, 'frame', [(i, i ^ k) for i in range(devices)])  31.9 us
    pallas_call x2, Pallas kernels, time_step(): pl.pallas_call(functools.partial(time_kernel, route, back, frames, slot),...  25.8 us
    ppermute x14, waiting for transfers between devices, exchange(): return lax.ppermute(block, 'frame', [(i, i ^ k) for i in range(devices)])  15.2 us
    all_to_all x2, starting transfers between devices, exchange_all(): return lax.all_to_all(block, 'frame', 0, 0, tiled=True)  12.2 us
    pallas_call x2, Pallas kernels, pack_step(): pl.pallas_call(functools.partial(pack_kernel, route, slot), in_specs=[pl....  6.08 us
  transfers between devices with their start and end apart: 16, of which 5 were waited for; matrix products, arithmetic and copies ran while one was open for 0% of the time, Pallas kernels for 26%

profile of v2, /device:TPU:0, one launch (start us, length us, event | category | flops | bytes accessed | tf_op | source)
XLA Modules:
  0.0 179.0 jit_solution(15386976817933327644)
XLA Ops:
  0.0 3.1 %pack_tokens.3 = bf16[8,4,32,1024]{3,2,1,0:T(8,128)(2,1)} custom-call(s32[2]{0:T(128)} %frame_count.7, bf16[2,4,256,1024]{3,2,1,0:T(8,128)(2,1)} %x_ref.7), custom_call_target="tpu_custom_call" | custom-call | tf_op jit(solution)/shard_map/pack_tokens/pallas_call | solution.py:262
  3.1 7.3 %all-to-all-start = ((bf16[8,4,32,1024]{3,2,1,0:T(8,128)(2,1)}), bf16[8,4,32,1024]{3,2,1,0:T(8,128)(2,1)S(1)}, u32[]{:S(2)}, u32[]{:S(2)}) async-start(bf16[8,4,32,1024]{3,2,1,0:T(8,128)(2,1)} %pack_tokens.3), calls=%async_computation | async-start | bytes 4194304 | tf_op jit(solution)/shard_map/all_to_all | solution.py:278
  10.4 3.0 %pack_tokens.2 = (bf16[4,32,1024]{2,1,0:T(8,128)(2,1)}, bf16[4,32,1024]{2,1,0:T(8,128)(2,1)}, bf16[4,32,1024]{2,1,0:T(8,128)(2,1)}, bf16[4,32,1024]{2,1,0:T(8,12...) custom-call(s32[2]{0:T(128)} %frame_count.7, ...), custom_call_target="tpu_custom_call" | custom-call | tf_op jit(solution)/shard_map/pack_tokens/pallas_call | solution.py:262
  13.4 45.2 %all-to-all-done.refs_0_ = bf16[8,4,32,1024]{3,2,1,0:T(8,128)(2,1)S(1)} async-done(((bf16[8,4,32,1024]{3,2,1,0:T(8,128)(2,1)}), bf16[8,4,32,1024]{3,2,1,0:T(8,128)(2,1)S(1)}, u32[]{:S(2)}, u32[]{:S(2)}) %all-to-all-start) | async-done | bytes 2097184 | tf_op jit(solution)/shard_map/all_to_all | solution.py:278
  58.6 1.5 collective-permute-start
  60.1 2.0 %collective-permute-start.1 = (bf16[4,32,1024]{2,1,0:T(8,128)(2,1)}, bf16[4,32,1024]{2,1,0:T(8,128)(2,1)S(1)}, u32[]{:S(2)}, u32[]{:S(2)}) collective-permute-start(bf16[4,32,1024]{2,1,0:T(8,128)(2,1)} %get-tuple-element.43), channel_id=1, source_target_pairs={{0,2},{1,3},{2,0},{3,1},{4,6},{5,7},{6,4},{7,5},{8,10},{9,11},{10,... | collective-permute-start | bytes 786440 | tf_op jit(solution)/shard_map/ppermute | solution.py:282
  62.1 0.8 collective-permute-start.2
  62.9 3.0 %collective-permute-start.4 = (bf16[4,32,1024]{2,1,0:T(8,128)(2,1)}, bf16[4,32,1024]{2,1,0:T(8,128)(2,1)S(1)}, u32[]{:S(2)}, u32[]{:S(2)}) collective-permute-start(bf16[4,32,1024]{2,1,0:T(8,128)(2,1)} %get-tuple-element.46), channel_id=1, source_target_pairs={{0,5},{1,4},{2,7},{3,6},{4,1},{5,0},{6,3},{7,2},{8,13},{9,12},{10,... | collective-permute-start | bytes 786440 | tf_op jit(solution)/shard_map/ppermute | solution.py:282
  65.9 3.4 %collective-permute-start.5 = (bf16[4,32,1024]{2,1,0:T(8,128)(2,1)}, bf16[4,32,1024]{2,1,0:T(8,128)(2,1)S(1)}, u32[]{:S(2)}, u32[]{:S(2)}) collective-permute-start(bf16[4,32,1024]{2,1,0:T(8,128)(2,1)} %get-tuple-element.47), channel_id=1, source_target_pairs={{0,6},{1,7},{2,4},{3,5},{4,2},{5,3},{6,0},{7,1},{8,14},{9,15},{10,... | collective-permute-start | bytes 786440 | tf_op jit(solution)/shard_map/ppermute | solution.py:282
  69.3 4.4 %collective-permute-done.3.refs_4_ = bf16[4,32,1024]{2,1,0:T(8,128)(2,1)S(1)} collective-permute-done((bf16[4,32,1024]{2,1,0:T(8,128)(2,1)}, bf16[4,32,1024]{2,1,0:T(8,128)(2,1)S(1)}, u32[]{:S(2)}, u32[]{:S(2)}) %collective-permute-start.3) | collective-permute-done | bytes 262176 | tf_op jit(solution)/shard_map/ppermute | solution.py:282
  73.8 1.1 collective-permute-start.6
  74.9 12.9 %time_attention.3 = (bf16[4,32,512]{2,1,0:T(8,128)(2,1)}, bf16[4,32,512]{2,1,0:T(8,128)(2,1)}, bf16[4,32,512]{2,1,0:T(8,128)(2,1)}, bf16[4,32,512]{2,1,0:T(8,128...) custom-call(s32[2]{0:T(128)} %frame_count.7, ...), custom_call_target="tpu_custom_call" | custom-call | flops 6442450944 | bytes 12000000 | tf_op jit(solution)/shard_map/time_attention/pallas_call | solution.py:141
  87.8 0.0 collective-permute-done.1.refs_2_
  87.8 0.0 copy-start.4
  87.8 0.1 collective-permute-start.7
  87.9 0.0 collective-permute-done.4.refs_5_
  87.9 3.7 %collective-permute-done.5.refs_6_ = bf16[4,32,1024]{2,1,0:T(8,128)(2,1)S(1)} collective-permute-done((bf16[4,32,1024]{2,1,0:T(8,128)(2,1)}, bf16[4,32,1024]{2,1,0:T(8,128)(2,1)S(1)}, u32[]{:S(2)}, u32[]{:S(2)}) %collective-permute-start.5) | collective-permute-done | bytes 262176 | tf_op jit(solution)/shard_map/ppermute | solution.py:282
  91.6 7.0 %collective-permute-done.6.refs_7_ = bf16[4,32,1024]{2,1,0:T(8,128)(2,1)S(1)} collective-permute-done((bf16[4,32,1024]{2,1,0:T(8,128)(2,1)}, bf16[4,32,1024]{2,1,0:T(8,128)(2,1)S(1)}, u32[]{:S(2)}, u32[]{:S(2)}) %collective-permute-start.6) | collective-permute-done | bytes 262176 | tf_op jit(solution)/shard_map/ppermute | solution.py:282
  98.6 13.0 %collective-permute-start.12 = (bf16[4,32,512]{2,1,0:T(8,128)(2,1)}, bf16[4,32,512]{2,1,0:T(8,128)(2,1)S(1)}, u32[]{:S(2)}, u32[]{:S(2)}) collective-permute-start(bf16[4,32,512]{2,1,0:T(8,128)(2,1)} %get-tuple-element.60), channel_id=1, source_target_pairs={{0,3},{1,2},{2,1},{3,0},{4,7},{5,6},{6,5},{7,4},{8,11},{9,10},{10,... | collective-permute-start | bytes 393224 | tf_op jit(solution)/shard_map/ppermute | solution.py:282
  111.7 1.4 collective-permute-start.11
  113.1 3.9 %collective-permute-start.9 = (bf16[4,32,512]{2,1,0:T(8,128)(2,1)}, bf16[4,32,512]{2,1,0:T(8,128)(2,1)S(1)}, u32[]{:S(2)}, u32[]{:S(2)}) collective-permute-start(bf16[4,32,512]{2,1,0:T(8,128)(2,1)} %get-tuple-element.54), channel_id=1, source_target_pairs={{0,5},{1,4},{2,7},{3,6},{4,1},{5,0},{6,3},{7,2},{8,13},{9,12},{10,... | collective-permute-start | bytes 393224 | tf_op jit(solution)/shard_map/ppermute | solution.py:282
  117.0 0.0 collective-permute-done.7.refs_4_
  117.0 0.6 collective-permute-start.8
  117.5 1.1 collective-permute-start.13
  118.7 12.9 %time_attention.2 = bf16[8,4,32,512]{3,2,1,0:T(8,128)(2,1)} custom-call(s32[2]{0:T(128)} %frame_count.7, bf16[2,4,256,1024]{3,2,1,0:T(8,128)(2,1)} %x_ref.7, bf16[4,32,1024]{2,1,0:T(8,128)(2,1)} %copy-done.2, bf16[4,32,1024]{2,1,0:T(8,128)(2,1)} %copy-done.4, bf16[4,32,1024]{2,1,0:T(8,128)(2,1)} %copy-done.5, bf16[4,32,1024]{2,1,0:T(8,128)(2,1)} %copy-done.3, ...), custom_call_target="tpu_custom_call" | custom-call | flops 6442450944 | bytes 12000000 | tf_op jit(solution)/shard_map/time_attention/pallas_call | solution.py:141
  131.6 0.0 collective-permute-done.10.refs_2_
  131.6 0.0 collective-permute-done.9.refs_5_
  131.7 4.9 %all-to-all-start.1 = ((bf16[8,4,32,512]{3,2,1,0:T(8,128)(2,1)}), bf16[8,4,32,512]{3,2,1,0:T(8,128)(2,1)S(1)}, u32[]{:S(2)}, u32[]{:S(2)}) async-start(bf16[8,4,32,512]{3,2,1,0:T(8,128)(2,1)} %time_attention.2), calls=%async_computation.1 | async-start | bytes 2097152 | tf_op jit(solution)/shard_map/all_to_all | solution.py:278
  136.6 17.2 %space_block.2.refs_5_ = bf16[2,4,256,1024]{3,2,1,0:T(8,128)(2,1)} custom-call(s32[2]{0:T(128)} %frame_count.7, s32[2]{0:T(128)} %token_count.3, bf16[2,4,256,1024]{3,2,1,0:T(8,128)(2,1)} %x_ref.7, bf16[4,32,512]{2,1,0:T(8,128)(2,1)} %get-tuple-element.64.refs_0_, bf16[4,32,512]{2,1,0:T(8,128)(2,1)} %copy-done.14, bf16[4,32,512]{2,1,0:T(8,128)(2,1)} %copy-done.12, ...), custom_call_target="tpu_custom_call" | custom-call | flops 10737418240 | bytes 8000000 | tf_op jit(solution)/shard_map/space_block/pallas_call | solution.py:211
  153.8 7.1 %all-to-all-done.1.refs_0_ = bf16[8,4,32,512]{3,2,1,0:T(8,128)(2,1)S(1)} async-done(((bf16[8,4,32,512]{3,2,1,0:T(8,128)(2,1)}), bf16[8,4,32,512]{3,2,1,0:T(8,128)(2,1)S(1)}, u32[]{:S(2)}, u32[]{:S(2)}) %all-to-all-start.1) | async-done | bytes 1048608 | tf_op jit(solution)/shard_map/all_to_all | solution.py:278
  161.0 1.0 copy-done.1
  162.0 17.1 %space_block.3 = bf16[2,4,256,1024]{3,2,1,0:T(8,128)(2,1)} custom-call(s32[2]{0:T(128)} %frame_count.7, s32[2]{0:T(128)} %token_count.3, bf16[2,4,256,1024]{3,2,1,0:T(8,128)(2,1)} %x_ref.7, bf16[8,4,32,512]{3,2,1,0:T(8,128)(2,1)} %copy-done.1, f32[1,1024]{1,0:T(1,128)} %bitcast.5, bf16[512,1024]{1,0:T(8,128)(2,1)} %refs_2_.3, ...), custom_call_target="tpu_custom_call", output_to_operand_aliasing={{}: (8, {})} | custom-call | flops 10737418240 | bytes 8000000 | tf_op jit(solution)/shard_map/space_block/pallas_call | solution.py:211
  (38 shorter events, 0.1 us)
Async XLA Ops:
  3.1 55.5 %all-to-all-start = ((bf16[8,4,32,1024]{3,2,1,0:T(8,128)(2,1)}), bf16[8,4,32,1024]{3,2,1,0:T(8,128)(2,1)S(1)}, u32[]{:S(2)}, u32[]{:S(2)}) async-start(bf16[8,4,32,1024]{3,2,1,0:T(8,128)(2,1)} %pack_tokens.3), calls=%async_computation | async-start | bytes 4194304 | tf_op jit(solution)/shard_map/all_to_all | solution.py:278
  58.6 16.3 %copy-start = (bf16[8,4,32,1024]{3,2,1,0:T(8,128)(2,1)}, bf16[8,4,32,1024]{3,2,1,0:T(8,128)(2,1)S(1)}, u32[]{:S(2)}) copy-start(bf16[8,4,32,1024]{3,2,1,0:T(8,128)(2,1)S(1)} %all-to-all-done.refs_0_) | copy-start | bytes 6291460
  58.6 7.3 %collective-permute-start = (bf16[4,32,1024]{2,1,0:T(8,128)(2,1)}, bf16[4,32,1024]{2,1,0:T(8,128)(2,1)S(1)}, u32[]{:S(2)}, u32[]{:S(2)}) collective-permute-start(bf16[4,32,1024]{2,1,0:T(8,128)(2,1)} %get-tuple-element.42), channel_id=1, source_target_pairs={{0,1},{1,0},{2,3},{3,2},{4,5},{5,4},{6,7},{7,6},{8,9},{9,8},{10,11... | collective-permute-start | bytes 786440 | tf_op jit(solution)/shard_map/ppermute | solution.py:282
  60.1 13.7 %collective-permute-start.3 = (bf16[4,32,1024]{2,1,0:T(8,128)(2,1)}, bf16[4,32,1024]{2,1,0:T(8,128)(2,1)S(1)}, u32[]{:S(2)}, u32[]{:S(2)}) collective-permute-start(bf16[4,32,1024]{2,1,0:T(8,128)(2,1)} %get-tuple-element.45), channel_id=1, source_target_pairs={{0,4},{1,5},{2,6},{3,7},{4,0},{5,1},{6,2},{7,3},{8,12},{9,13},{10,... | collective-permute-start | bytes 786440 | tf_op jit(solution)/shard_map/ppermute | solution.py:282
  60.1 27.7 %collective-permute-start.1 = (bf16[4,32,1024]{2,1,0:T(8,128)(2,1)}, bf16[4,32,1024]{2,1,0:T(8,128)(2,1)S(1)}, u32[]{:S(2)}, u32[]{:S(2)}) collective-permute-start(bf16[4,32,1024]{2,1,0:T(8,128)(2,1)} %get-tuple-element.43), channel_id=1, source_target_pairs={{0,2},{1,3},{2,0},{3,1},{4,6},{5,7},{6,4},{7,5},{8,10},{9,11},{10,... | collective-permute-start | bytes 786440 | tf_op jit(solution)/shard_map/ppermute | solution.py:282
  62.1 25.8 %collective-permute-start.2 = (bf16[4,32,1024]{2,1,0:T(8,128)(2,1)}, bf16[4,32,1024]{2,1,0:T(8,128)(2,1)S(1)}, u32[]{:S(2)}, u32[]{:S(2)}) collective-permute-start(bf16[4,32,1024]{2,1,0:T(8,128)(2,1)} %get-tuple-element.44), channel_id=1, source_target_pairs={{0,3},{1,2},{2,1},{3,0},{4,7},{5,6},{6,5},{7,4},{8,11},{9,10},{10,... | collective-permute-start | bytes 786440 | tf_op jit(solution)/shard_map/ppermute | solution.py:282
  62.9 25.0 %collective-permute-start.4 = (bf16[4,32,1024]{2,1,0:T(8,128)(2,1)}, bf16[4,32,1024]{2,1,0:T(8,128)(2,1)S(1)}, u32[]{:S(2)}, u32[]{:S(2)}) collective-permute-start(bf16[4,32,1024]{2,1,0:T(8,128)(2,1)} %get-tuple-element.46), channel_id=1, source_target_pairs={{0,5},{1,4},{2,7},{3,6},{4,1},{5,0},{6,3},{7,2},{8,13},{9,12},{10,... | collective-permute-start | bytes 786440 | tf_op jit(solution)/shard_map/ppermute | solution.py:282
  65.9 21.9 %copy-start.2 = (bf16[4,32,1024]{2,1,0:T(8,128)(2,1)}, bf16[4,32,1024]{2,1,0:T(8,128)(2,1)S(1)}, u32[]{:S(2)}) copy-start(bf16[4,32,1024]{2,1,0:T(8,128)(2,1)S(1)} %collective-permute-done.refs_1_) | copy-start | bytes 786436
  65.9 25.7 %collective-permute-start.5 = (bf16[4,32,1024]{2,1,0:T(8,128)(2,1)}, bf16[4,32,1024]{2,1,0:T(8,128)(2,1)S(1)}, u32[]{:S(2)}, u32[]{:S(2)}) collective-permute-start(bf16[4,32,1024]{2,1,0:T(8,128)(2,1)} %get-tuple-element.47), channel_id=1, source_target_pairs={{0,6},{1,7},{2,4},{3,5},{4,2},{5,3},{6,0},{7,1},{8,14},{9,15},{10,... | collective-permute-start | bytes 786440 | tf_op jit(solution)/shard_map/ppermute | solution.py:282
  73.8 14.0 %copy-start.3 = (bf16[4,32,1024]{2,1,0:T(8,128)(2,1)}, bf16[4,32,1024]{2,1,0:T(8,128)(2,1)S(1)}, u32[]{:S(2)}) copy-start(bf16[4,32,1024]{2,1,0:T(8,128)(2,1)S(1)} %collective-permute-done.3.refs_4_) | copy-start | bytes 786436
  73.8 24.9 %collective-permute-start.6 = (bf16[4,32,1024]{2,1,0:T(8,128)(2,1)}, bf16[4,32,1024]{2,1,0:T(8,128)(2,1)S(1)}, u32[]{:S(2)}, u32[]{:S(2)}) collective-permute-start(bf16[4,32,1024]{2,1,0:T(8,128)(2,1)} %get-tuple-element.48), channel_id=1, source_target_pairs={{0,7},{1,6},{2,5},{3,4},{4,3},{5,2},{6,1},{7,0},{8,15},{9,14},{10,... | collective-permute-start | bytes 786440 | tf_op jit(solution)/shard_map/ppermute | solution.py:282
  87.8 30.9 %copy-start.4 = (bf16[4,32,1024]{2,1,0:T(8,128)(2,1)}, bf16[4,32,1024]{2,1,0:T(8,128)(2,1)S(1)}, u32[]{:S(2)}) copy-start(bf16[4,32,1024]{2,1,0:T(8,128)(2,1)S(1)} %collective-permute-done.1.refs_2_) | copy-start | bytes 786436
  87.8 29.1 %collective-permute-start.7 = (bf16[4,32,512]{2,1,0:T(8,128)(2,1)}, bf16[4,32,512]{2,1,0:T(8,128)(2,1)S(1)}, u32[]{:S(2)}, u32[]{:S(2)}) collective-permute-start(bf16[4,32,512]{2,1,0:T(8,128)(2,1)} %get-tuple-element.50), channel_id=1, source_target_pairs={{0,4},{1,5},{2,6},{3,7},{4,0},{5,1},{6,2},{7,3},{8,12},{9,13},{10,... | collective-permute-start | bytes 393224 | tf_op jit(solution)/shard_map/ppermute | solution.py:282
  87.9 30.8 %copy-start.5 = (bf16[4,32,1024]{2,1,0:T(8,128)(2,1)}, bf16[4,32,1024]{2,1,0:T(8,128)(2,1)S(1)}, u32[]{:S(2)}) copy-start(bf16[4,32,1024]{2,1,0:T(8,128)(2,1)S(1)} %collective-permute-done.2.refs_3_) | copy-start | bytes 786436
  87.9 30.7 %copy-start.6 = (bf16[4,32,1024]{2,1,0:T(8,128)(2,1)}, bf16[4,32,1024]{2,1,0:T(8,128)(2,1)S(1)}, u32[]{:S(2)}) copy-start(bf16[4,32,1024]{2,1,0:T(8,128)(2,1)S(1)} %collective-permute-done.4.refs_5_) | copy-start | bytes 786436
  91.6 27.1 %copy-start.7 = (bf16[4,32,1024]{2,1,0:T(8,128)(2,1)}, bf16[4,32,1024]{2,1,0:T(8,128)(2,1)S(1)}, u32[]{:S(2)}) copy-start(bf16[4,32,1024]{2,1,0:T(8,128)(2,1)S(1)} %collective-permute-done.5.refs_6_) | copy-start | bytes 786436
  98.6 20.0 %copy-start.8 = (bf16[4,32,1024]{2,1,0:T(8,128)(2,1)}, bf16[4,32,1024]{2,1,0:T(8,128)(2,1)S(1)}, u32[]{:S(2)}) copy-start(bf16[4,32,1024]{2,1,0:T(8,128)(2,1)S(1)} %collective-permute-done.6.refs_7_) | copy-start | bytes 786436
  98.6 18.9 %collective-permute-start.12 = (bf16[4,32,512]{2,1,0:T(8,128)(2,1)}, bf16[4,32,512]{2,1,0:T(8,128)(2,1)S(1)}, u32[]{:S(2)}, u32[]{:S(2)}) collective-permute-start(bf16[4,32,512]{2,1,0:T(8,128)(2,1)} %get-tuple-element.60), channel_id=1, source_target_pairs={{0,3},{1,2},{2,1},{3,0},{4,7},{5,6},{6,5},{7,4},{8,11},{9,10},{10,... | collective-permute-start | bytes 393224 | tf_op jit(solution)/shard_map/ppermute | solution.py:282
  111.7 19.9 %collective-permute-start.11 = (bf16[4,32,512]{2,1,0:T(8,128)(2,1)}, bf16[4,32,512]{2,1,0:T(8,128)(2,1)S(1)}, u32[]{:S(2)}, u32[]{:S(2)}) collective-permute-start(bf16[4,32,512]{2,1,0:T(8,128)(2,1)} %get-tuple-element.58), channel_id=1, source_target_pairs={{0,6},{1,7},{2,4},{3,5},{4,2},{5,3},{6,0},{7,1},{8,14},{9,15},{10,... | collective-permute-start | bytes 393224 | tf_op jit(solution)/shard_map/ppermute | solution.py:282
  113.1 18.5 %collective-permute-start.10 = (bf16[4,32,512]{2,1,0:T(8,128)(2,1)}, bf16[4,32,512]{2,1,0:T(8,128)(2,1)S(1)}, u32[]{:S(2)}, u32[]{:S(2)}) collective-permute-start(bf16[4,32,512]{2,1,0:T(8,128)(2,1)} %get-tuple-element.56), channel_id=1, source_target_pairs={{0,2},{1,3},{2,0},{3,1},{4,6},{5,7},{6,4},{7,5},{8,10},{9,11},{10,... | collective-permute-start | bytes 393224 | tf_op jit(solution)/shard_map/ppermute | solution.py:282
  113.1 18.5 %collective-permute-start.9 = (bf16[4,32,512]{2,1,0:T(8,128)(2,1)}, bf16[4,32,512]{2,1,0:T(8,128)(2,1)S(1)}, u32[]{:S(2)}, u32[]{:S(2)}) collective-permute-start(bf16[4,32,512]{2,1,0:T(8,128)(2,1)} %get-tuple-element.54), channel_id=1, source_target_pairs={{0,5},{1,4},{2,7},{3,6},{4,1},{5,0},{6,3},{7,2},{8,13},{9,12},{10,... | collective-permute-start | bytes 393224 | tf_op jit(solution)/shard_map/ppermute | solution.py:282
  117.0 14.6 %copy-start.9 = (bf16[4,32,512]{2,1,0:T(8,128)(2,1)}, bf16[4,32,512]{2,1,0:T(8,128)(2,1)S(1)}, u32[]{:S(2)}) copy-start(bf16[4,32,512]{2,1,0:T(8,128)(2,1)S(1)} %collective-permute-done.7.refs_4_) | copy-start | bytes 393220
  117.0 14.7 %collective-permute-start.8 = (bf16[4,32,512]{2,1,0:T(8,128)(2,1)}, bf16[4,32,512]{2,1,0:T(8,128)(2,1)S(1)}, u32[]{:S(2)}, u32[]{:S(2)}) collective-permute-start(bf16[4,32,512]{2,1,0:T(8,128)(2,1)} %get-tuple-element.52), channel_id=1, source_target_pairs={{0,1},{1,0},{2,3},{3,2},{4,5},{5,4},{6,7},{7,6},{8,9},{9,8},{10,11... | collective-permute-start | bytes 393224 | tf_op jit(solution)/shard_map/ppermute | solution.py:282
  117.5 14.0 %copy-start.10 = (bf16[4,32,512]{2,1,0:T(8,128)(2,1)}, bf16[4,32,512]{2,1,0:T(8,128)(2,1)S(1)}, u32[]{:S(2)}) copy-start(bf16[4,32,512]{2,1,0:T(8,128)(2,1)S(1)} %collective-permute-done.12.refs_3_) | copy-start | bytes 393220
  117.5 14.1 %collective-permute-start.13 = (bf16[4,32,512]{2,1,0:T(8,128)(2,1)}, bf16[4,32,512]{2,1,0:T(8,128)(2,1)S(1)}, u32[]{:S(2)}, u32[]{:S(2)}) collective-permute-start(bf16[4,32,512]{2,1,0:T(8,128)(2,1)} %get-tuple-element.62), channel_id=1, source_target_pairs={{0,7},{1,6},{2,5},{3,4},{4,3},{5,2},{6,1},{7,0},{8,15},{9,14},{10,... | collective-permute-start | bytes 393224 | tf_op jit(solution)/shard_map/ppermute | solution.py:282
  131.6 5.0 %copy-start.11 = (bf16[4,32,512]{2,1,0:T(8,128)(2,1)}, bf16[4,32,512]{2,1,0:T(8,128)(2,1)S(1)}, u32[]{:S(2)}) copy-start(bf16[4,32,512]{2,1,0:T(8,128)(2,1)S(1)} %collective-permute-done.11.refs_6_) | copy-start | bytes 393220
  131.6 5.0 %copy-start.12 = (bf16[4,32,512]{2,1,0:T(8,128)(2,1)}, bf16[4,32,512]{2,1,0:T(8,128)(2,1)S(1)}, u32[]{:S(2)}) copy-start(bf16[4,32,512]{2,1,0:T(8,128)(2,1)S(1)} %collective-permute-done.10.refs_2_) | copy-start | bytes 393220
  131.6 5.0 %copy-start.13 = (bf16[4,32,512]{2,1,0:T(8,128)(2,1)}, bf16[4,32,512]{2,1,0:T(8,128)(2,1)S(1)}, u32[]{:S(2)}) copy-start(bf16[4,32,512]{2,1,0:T(8,128)(2,1)S(1)} %collective-permute-done.9.refs_5_) | copy-start | bytes 393220
  131.7 5.0 %copy-start.14 = (bf16[4,32,512]{2,1,0:T(8,128)(2,1)}, bf16[4,32,512]{2,1,0:T(8,128)(2,1)S(1)}, u32[]{:S(2)}) copy-start(bf16[4,32,512]{2,1,0:T(8,128)(2,1)S(1)} %collective-permute-done.8.refs_1_) | copy-start | bytes 393220
  131.7 4.9 %copy-start.15 = (bf16[4,32,512]{2,1,0:T(8,128)(2,1)}, bf16[4,32,512]{2,1,0:T(8,128)(2,1)S(1)}, u32[]{:S(2)}) copy-start(bf16[4,32,512]{2,1,0:T(8,128)(2,1)S(1)} %collective-permute-done.13.refs_7_) | copy-start | bytes 393220
  131.7 29.3 %all-to-all-start.1 = ((bf16[8,4,32,512]{3,2,1,0:T(8,128)(2,1)}), bf16[8,4,32,512]{3,2,1,0:T(8,128)(2,1)S(1)}, u32[]{:S(2)}, u32[]{:S(2)}) async-start(bf16[8,4,32,512]{3,2,1,0:T(8,128)(2,1)} %time_attention.2), calls=%async_computation.1 | async-start | bytes 2097152 | tf_op jit(solution)/shard_map/all_to_all | solution.py:278
  161.0 1.0 copy-start.1

commit v3 on v2

--- a/solution.py
+++ b/solution.py
@@ -12,6 +12,7 @@
 HW = 512
 ROWS = 16
 NEG = -1e30
+PER = 2
 LEAD = 2
 TAIL = 7
 VMEM_LIMIT = 56 * 1024 * 1024
@@ -32,18 +33,22 @@
     count = rows.size
     low = lax.broadcasted_iota(jnp.int32, (count, 2 * HD), 1) < HD
     zero = jnp.zeros((count, 2 * HD), jnp.bfloat16)
+    scores = []
     for pair in range(HEADS // 2):
         cols = pair * 2 * HD
         q = qkv_ref[rows, cols : cols + 2 * HD]
         k = qkv_ref[rows, HW + cols : HW + cols + 2 * HD]
+        for keys in (jnp.where(low, k, zero), jnp.where(low, zero, k)):
+            scores.append(lax.dot_general(q, keys, (((1,), (1,)), ((), ())), preferred_element_type=jnp.float32))
+    weights = []
+    for score in scores:
+        score = score + bias
+        expo = jnp.exp(score - jnp.max(score, axis=-1, keepdims=True))
+        weights.append((expo * (1.0 / jnp.sum(expo, axis=-1, keepdims=True))).astype(jnp.bfloat16))
+    for pair in range(HEADS // 2):
+        cols = pair * 2 * HD
         v = qkv_ref[rows, 2 * HW + cols : 2 * HW + cols + 2 * HD]
-        parts = []
-        for keys in (jnp.where(low, k, zero), jnp.where(low, zero, k)):
-            scores = lax.dot_general(q, keys, (((1,), (1,)), ((), ())), preferred_element_type=jnp.float32)
-            scores = scores + bias
-            expo = jnp.exp(scores - jnp.max(scores, axis=-1, keepdims=True))
-            weights = (expo * (1.0 / jnp.sum(expo, axis=-1, keepdims=True))).astype(jnp.bfloat16)
-            parts.append(jnp.dot(weights, v, preferred_element_type=jnp.float32))
+        parts = [jnp.dot(weights[2 * pair + j], v, preferred_element_type=jnp.float32) for j in range(2)]
         out_ref[rows, cols : cols + 2 * HD] = jnp.where(low, parts[0], parts[1]).astype(jnp.bfloat16)
 
 
@@ -100,7 +105,9 @@
         for s in range(ROWS // 8):
             piece = normed[:, s * 8 : s * 8 + 8, :].reshape(group, normed.shape[-1])
             normed_ref[s * half + k * group : s * half + (k + 1) * group, :] = normalise(piece, gain)
-    project_heads(normed_ref[...], weight_ref, qkv_ref)
+    for s in range(ROWS // 8):
+        rows = pl.ds(s * half, half)
+        project_heads(normed_ref[rows, :], weight_ref, qkv_ref.at[rows])
     for s in range(ROWS // 8):
         attend(qkv_ref, pl.ds(s * half, half), bias_ref[...], att_ref)
     for k in range(devices):
@@ -161,36 +168,44 @@
     )(frame_count, *operands, gain, weight)
 
 
-def space_kernel(route, frames, slot, first, aliased, frame_count, token_count, x_ref, *refs):
+def space_kernel(route, frames, slot, first, per, aliased, frame_count, token_count, x_ref, *refs):
     devices, count = route.devices, route.count
     n_in = 1 if route.whole else devices
     pieces = refs[:n_in]
     gain_ref, time_out_ref, weight_ref, space_out_ref = refs[n_in : n_in + 4]
-    out_ref, att_ref, mid_ref, qkv_ref = refs[n_in + 4 + aliased :]
+    out_ref = refs[n_in + 4 + aliased]
+    scratch = refs[n_in + 5 + aliased :]
     tokens = x_ref.shape[2]
     me = lax.axis_index("frame")
     clip = clip_at(slot, frame_count)
     token_end = token_count[clip]
-    live = me * frames + first + pl.program_id(0) < frame_count[clip]
+    begin = me * frames + first + pl.program_id(0) * per
+    live = begin < frame_count[clip]
 
     @pl.when(live)
     def _():
-        for k in range(devices):
-            start = pl.multiple_of(block_start(route.peer(me, k), count, tokens), ROWS)
-            att_ref[pl.ds(start, count), :] = pieces[0][k, 0] if route.whole else pieces[k][0]
-        mid = x_ref[0, 0].astype(jnp.float32) + jnp.dot(
+        bias = jnp.where(lax.broadcasted_iota(jnp.int32, (1, tokens), 1) < token_end, 0.0, NEG).astype(jnp.float32)
+        place = lax.broadcasted_iota(jnp.int32, (tokens, 1), 0)
+        att_ref, mid_ref, qkv_ref = scratch
+        for f in range(per):
+            for k in range(devices):
+                start = pl.multiple_of(block_start(route.peer(me, k), count, tokens), ROWS) + f * tokens
+                att_ref[pl.ds(start, count), :] = pieces[0][k, f] if route.whole else pieces[k][f]
+        mid = x_ref[0].reshape(per * tokens, -1).astype(jnp.float32) + jnp.dot(
             att_ref[...], time_out_ref[...], preferred_element_type=jnp.float32
         )
         mid_ref[...] = mid.astype(jnp.bfloat16)
-        normed = normalise(mid_ref[...].astype(jnp.float32), gain_ref[...])
-        project_heads(normed, weight_ref, qkv_ref)
-        bias = jnp.where(lax.broadcasted_iota(jnp.int32, (1, tokens), 1) < token_end, 0.0, NEG).astype(jnp.float32)
-        attend(qkv_ref, pl.ds(0, tokens), bias, att_ref)
+        for f in range(per):
+            rows = pl.ds(f * tokens, tokens)
+            project_heads(normalise(mid_ref[rows, :].astype(jnp.float32), gain_ref[...]), weight_ref, qkv_ref.at[rows])
+        for f in range(per):
+            attend(qkv_ref, pl.ds(f * tokens, tokens), bias, att_ref)
         result = mid_ref[...].astype(jnp.float32) + jnp.dot(
             att_ref[...], space_out_ref[...], preferred_element_type=jnp.float32
         )
-        keep = lax.broadcasted_iota(jnp.int32, (tokens, 1), 0) < token_end
-        out_ref[0, 0] = jnp.where(keep, result, 0.0).astype(jnp.bfloat16)
+        for f in range(per):
+            keep = (place < token_end) & (begin + f < frame_count[clip])
+            out_ref[0, f] = jnp.where(keep, result[f * tokens : (f + 1) * tokens], 0.0).astype(jnp.bfloat16)
 
     @pl.when(jnp.logical_not(live))
     def _():
@@ -200,25 +215,26 @@
 def space_step(route, slot, counts, tokens, pieces, offset, first, calls, weights, partial):
     _, frames, places, width = tokens.shape
     devices, count = route.devices, route.count
-    skip = first - offset
-    unit = pl.BlockSpec((1, 1, places, width), lambda i, c, t: (clip_at(slot, c), first + i, 0, 0))
+    per = PER if calls % PER == 0 and first % PER == 0 and offset % PER == 0 else 1
+    skip = (first - offset) // per
+    unit = pl.BlockSpec((1, per, places, width), lambda i, c, t: (clip_at(slot, c), first // per + i, 0, 0))
     if route.whole:
-        piece_specs = [pl.BlockSpec((devices, 1, count, HW), lambda i, *_: (0, skip + i, 0, 0))]
+        piece_specs = [pl.BlockSpec((devices, per, count, HW), lambda i, *_: (0, skip + i, 0, 0))]
     else:
-        piece_specs = [pl.BlockSpec((1, count, HW), lambda i, *_: (skip + i, 0, 0))] * devices
+        piece_specs = [pl.BlockSpec((per, count, HW), lambda i, *_: (skip + i, 0, 0))] * devices
     aliased = partial is not None
     operands = [*counts, tokens, *pieces, *weights] + ([partial] if aliased else [])
     return pl.pallas_call(
-        functools.partial(space_kernel, route, frames, slot, first, int(aliased)),
+        functools.partial(space_kernel, route, frames, slot, first, per, int(aliased)),
         grid_spec=pltpu.PrefetchScalarGridSpec(
             num_scalar_prefetch=2,
-            grid=(calls,),
+            grid=(calls // per,),
             in_specs=[unit] + piece_specs + [KEPT(a) for a in weights] + ([ANY] if aliased else []),
             out_specs=unit,
             scratch_shapes=[
-                pltpu.VMEM((places, HW), jnp.bfloat16),
-                pltpu.VMEM((places, width), jnp.bfloat16),
-                pltpu.VMEM((places, 3 * HW), jnp.bfloat16),
+                pltpu.VMEM((per * places, HW), jnp.bfloat16),
+                pltpu.VMEM((per * places, width), jnp.bfloat16),
+                pltpu.VMEM((per * places, 3 * HW), jnp.bfloat16),
             ],
         ),
         out_shape=jax.ShapeDtypeStruct(tokens.shape, jnp.bfloat16),

time: 179 us -> 176 us (0.983)
  Pallas kernels: 66.1 us -> 58.7 us
  waiting for transfers between devices: 67.5 us -> 71.2 us
    pallas_call x2, Pallas kernels: 34.3 us -> 29.3 us  [space_step(): pl.pallas_call(functools.partial(space_kernel, route, frames, slot, first...]
    pallas_call x2, Pallas kernels: 25.8 us -> 23.3 us  [time_step(): pl.pallas_call(functools.partial(time_kernel, route, back, frames, slot),...]
    all_to_all x2, waiting for transfers between devices: 52.3 us -> 54.8 us  [exchange_all(): return lax.all_to_all(block, 'frame', 0, 0, tiled=True)]
  transfers between devices with their start and end apart: 16 -> 16, of which waited for: 5 -> 5; matrix products, arithmetic and copies ran while one was open for 0% -> 0% of each run, Pallas kernels for 26% -> 23%
where the time goes in v3:
time: 176 us; the launch traced here: 175 us
  waiting for transfers between devices  71.2 us (40%)
  Pallas kernels  58.7 us (33%)
  starting transfers between devices  44.1 us (25%)
    all_to_all x2, waiting for transfers between devices, exchange_all(): return lax.all_to_all(block, 'frame', 0, 0, tiled=True)  54.8 us
    ppermute x14, starting transfers between devices, exchange(): return lax.ppermute(block, 'frame', [(i, i ^ k) for i in range(devices)])  31.9 us
    pallas_call x2, Pallas kernels, space_step(): pl.pallas_call(functools.partial(space_kernel, route, frames, slot, first...  29.3 us
    pallas_call x2, Pallas kernels, time_step(): pl.pallas_call(functools.partial(time_kernel, route, back, frames, slot),...  23.3 us
    ppermute x14, waiting for transfers between devices, exchange(): return lax.ppermute(block, 'frame', [(i, i ^ k) for i in range(devices)])  16.4 us
    all_to_all x2, starting transfers between devices, exchange_all(): return lax.all_to_all(block, 'frame', 0, 0, tiled=True)  12.2 us
    pallas_call x2, Pallas kernels, pack_step(): pl.pallas_call(functools.partial(pack_kernel, route, slot), in_specs=[pl....  6.08 us
  transfers between devices with their start and end apart: 16, of which 5 were waited for; matrix products, arithmetic and copies ran while one was open for 0% of the time, Pallas kernels for 23%

profile of v3, /device:TPU:0, one launch (start us, length us, event | category | flops | bytes accessed | tf_op | source)
XLA Modules:
  0.0 175.3 jit_solution(6010690199263424502)
XLA Ops:
  0.0 3.1 %pack_tokens.3 = bf16[8,4,32,1024]{3,2,1,0:T(8,128)(2,1)} custom-call(s32[2]{0:T(128)} %frame_count.7, bf16[2,4,256,1024]{3,2,1,0:T(8,128)(2,1)} %x_ref.7), custom_call_target="tpu_custom_call" | custom-call | tf_op jit(solution)/shard_map/pack_tokens/pallas_call | solution.py:278
  3.1 7.3 %all-to-all-start = ((bf16[8,4,32,1024]{3,2,1,0:T(8,128)(2,1)}), bf16[8,4,32,1024]{3,2,1,0:T(8,128)(2,1)S(1)}, u32[]{:S(2)}, u32[]{:S(2)}) async-start(bf16[8,4,32,1024]{3,2,1,0:T(8,128)(2,1)} %pack_tokens.3), calls=%async_computation | async-start | bytes 4194304 | tf_op jit(solution)/shard_map/all_to_all | solution.py:294
  10.4 3.0 %pack_tokens.2 = (bf16[4,32,1024]{2,1,0:T(8,128)(2,1)}, bf16[4,32,1024]{2,1,0:T(8,128)(2,1)}, bf16[4,32,1024]{2,1,0:T(8,128)(2,1)}, bf16[4,32,1024]{2,1,0:T(8,12...) custom-call(s32[2]{0:T(128)} %frame_count.7, ...), custom_call_target="tpu_custom_call" | custom-call | tf_op jit(solution)/shard_map/pack_tokens/pallas_call | solution.py:278
  13.4 45.2 %all-to-all-done.refs_0_ = bf16[8,4,32,1024]{3,2,1,0:T(8,128)(2,1)S(1)} async-done(((bf16[8,4,32,1024]{3,2,1,0:T(8,128)(2,1)}), bf16[8,4,32,1024]{3,2,1,0:T(8,128)(2,1)S(1)}, u32[]{:S(2)}, u32[]{:S(2)}) %all-to-all-start) | async-done | bytes 2097184 | tf_op jit(solution)/shard_map/all_to_all | solution.py:294
  58.6 1.5 collective-permute-start
  60.1 0.0 collective-permute-start.3
  60.1 2.0 %collective-permute-start.1 = (bf16[4,32,1024]{2,1,0:T(8,128)(2,1)}, bf16[4,32,1024]{2,1,0:T(8,128)(2,1)S(1)}, u32[]{:S(2)}, u32[]{:S(2)}) collective-permute-start(bf16[4,32,1024]{2,1,0:T(8,128)(2,1)} %get-tuple-element.43), channel_id=1, source_target_pairs={{0,2},{1,3},{2,0},{3,1},{4,6},{5,7},{6,4},{7,5},{8,10},{9,11},{10,... | collective-permute-start | bytes 786440 | tf_op jit(solution)/shard_map/ppermute | solution.py:298
  62.1 0.8 collective-permute-start.2
  62.9 3.0 %collective-permute-start.4 = (bf16[4,32,1024]{2,1,0:T(8,128)(2,1)}, bf16[4,32,1024]{2,1,0:T(8,128)(2,1)S(1)}, u32[]{:S(2)}, u32[]{:S(2)}) collective-permute-start(bf16[4,32,1024]{2,1,0:T(8,128)(2,1)} %get-tuple-element.46), channel_id=1, source_target_pairs={{0,5},{1,4},{2,7},{3,6},{4,1},{5,0},{6,3},{7,2},{8,13},{9,12},{10,... | collective-permute-start | bytes 786440 | tf_op jit(solution)/shard_map/ppermute | solution.py:298
  65.9 0.0 collective-permute-done.refs_1_
  65.9 3.4 %collective-permute-start.5 = (bf16[4,32,1024]{2,1,0:T(8,128)(2,1)}, bf16[4,32,1024]{2,1,0:T(8,128)(2,1)S(1)}, u32[]{:S(2)}, u32[]{:S(2)}) collective-permute-start(bf16[4,32,1024]{2,1,0:T(8,128)(2,1)} %get-tuple-element.47), channel_id=1, source_target_pairs={{0,6},{1,7},{2,4},{3,5},{4,2},{5,3},{6,0},{7,1},{8,14},{9,15},{10,... | collective-permute-start | bytes 786440 | tf_op jit(solution)/shard_map/ppermute | solution.py:298
  69.3 4.4 %collective-permute-done.3.refs_4_ = bf16[4,32,1024]{2,1,0:T(8,128)(2,1)S(1)} collective-permute-done((bf16[4,32,1024]{2,1,0:T(8,128)(2,1)}, bf16[4,32,1024]{2,1,0:T(8,128)(2,1)S(1)}, u32[]{:S(2)}, u32[]{:S(2)}) %collective-permute-start.3) | collective-permute-done | bytes 262176 | tf_op jit(solution)/shard_map/ppermute | solution.py:298
  73.8 1.1 collective-permute-start.6
  74.9 11.7 %time_attention.3 = (bf16[4,32,512]{2,1,0:T(8,128)(2,1)}, bf16[4,32,512]{2,1,0:T(8,128)(2,1)}, bf16[4,32,512]{2,1,0:T(8,128)(2,1)}, bf16[4,32,512]{2,1,0:T(8,128...) custom-call(s32[2]{0:T(128)} %frame_count.7, ...), custom_call_target="tpu_custom_call" | custom-call | flops 6442450944 | bytes 12000000 | tf_op jit(solution)/shard_map/time_attention/pallas_call | solution.py:148
  86.6 0.0 collective-permute-done.1.refs_2_
  86.6 0.0 copy-start.4
  86.6 0.1 collective-permute-start.7
  86.7 0.0 collective-permute-done.2.refs_3_
  86.7 0.0 collective-permute-done.4.refs_5_
  86.7 4.9 %collective-permute-done.5.refs_6_ = bf16[4,32,1024]{2,1,0:T(8,128)(2,1)S(1)} collective-permute-done((bf16[4,32,1024]{2,1,0:T(8,128)(2,1)}, bf16[4,32,1024]{2,1,0:T(8,128)(2,1)S(1)}, u32[]{:S(2)}, u32[]{:S(2)}) %collective-permute-start.5) | collective-permute-done | bytes 262176 | tf_op jit(solution)/shard_map/ppermute | solution.py:298
  91.6 7.0 %collective-permute-done.6.refs_7_ = bf16[4,32,1024]{2,1,0:T(8,128)(2,1)S(1)} collective-permute-done((bf16[4,32,1024]{2,1,0:T(8,128)(2,1)}, bf16[4,32,1024]{2,1,0:T(8,128)(2,1)S(1)}, u32[]{:S(2)}, u32[]{:S(2)}) %collective-permute-start.6) | collective-permute-done | bytes 262176 | tf_op jit(solution)/shard_map/ppermute | solution.py:298
  98.6 13.0 %collective-permute-start.12 = (bf16[4,32,512]{2,1,0:T(8,128)(2,1)}, bf16[4,32,512]{2,1,0:T(8,128)(2,1)S(1)}, u32[]{:S(2)}, u32[]{:S(2)}) collective-permute-start(bf16[4,32,512]{2,1,0:T(8,128)(2,1)} %get-tuple-element.60), channel_id=1, source_target_pairs={{0,3},{1,2},{2,1},{3,0},{4,7},{5,6},{6,5},{7,4},{8,11},{9,10},{10,... | collective-permute-start | bytes 393224 | tf_op jit(solution)/shard_map/ppermute | solution.py:298
  111.7 1.4 collective-permute-start.11
  113.1 3.9 %collective-permute-start.9 = (bf16[4,32,512]{2,1,0:T(8,128)(2,1)}, bf16[4,32,512]{2,1,0:T(8,128)(2,1)S(1)}, u32[]{:S(2)}, u32[]{:S(2)}) collective-permute-start(bf16[4,32,512]{2,1,0:T(8,128)(2,1)} %get-tuple-element.54), channel_id=1, source_target_pairs={{0,5},{1,4},{2,7},{3,6},{4,1},{5,0},{6,3},{7,2},{8,13},{9,12},{10,... | collective-permute-start | bytes 393224 | tf_op jit(solution)/shard_map/ppermute | solution.py:298
  117.0 0.6 collective-permute-start.8
  117.5 1.1 collective-permute-start.13
  118.7 11.6 %time_attention.2 = bf16[8,4,32,512]{3,2,1,0:T(8,128)(2,1)} custom-call(s32[2]{0:T(128)} %frame_count.7, bf16[2,4,256,1024]{3,2,1,0:T(8,128)(2,1)} %x_ref.7, bf16[4,32,1024]{2,1,0:T(8,128)(2,1)} %copy-done.2, bf16[4,32,1024]{2,1,0:T(8,128)(2,1)} %copy-done.4, bf16[4,32,1024]{2,1,0:T(8,128)(2,1)} %copy-done.5, bf16[4,32,1024]{2,1,0:T(8,128)(2,1)} %copy-done.3, ...), custom_call_target="tpu_custom_call" | custom-call | flops 6442450944 | bytes 12000000 | tf_op jit(solution)/shard_map/time_attention/pallas_call | solution.py:148
  130.4 4.9 %all-to-all-start.1 = ((bf16[8,4,32,512]{3,2,1,0:T(8,128)(2,1)}), bf16[8,4,32,512]{3,2,1,0:T(8,128)(2,1)S(1)}, u32[]{:S(2)}, u32[]{:S(2)}) async-start(bf16[8,4,32,512]{3,2,1,0:T(8,128)(2,1)} %time_attention.2), calls=%async_computation.1 | async-start | bytes 2097152 | tf_op jit(solution)/shard_map/all_to_all | solution.py:294
  135.4 14.8 %space_block.2.refs_5_ = bf16[2,4,256,1024]{3,2,1,0:T(8,128)(2,1)} custom-call(s32[2]{0:T(128)} %frame_count.7, s32[2]{0:T(128)} %token_count.3, bf16[2,4,256,1024]{3,2,1,0:T(8,128)(2,1)} %x_ref.7, bf16[4,32,512]{2,1,0:T(8,128)(2,1)} %get-tuple-element.64.refs_0_, bf16[4,32,512]{2,1,0:T(8,128)(2,1)} %copy-done.14, bf16[4,32,512]{2,1,0:T(8,128)(2,1)} %copy-done.12, ...), custom_call_target="tpu_custom_call" | custom-call | flops 10737418240 | bytes 8000000 | tf_op jit(solution)/shard_map/space_block/pallas_call | solution.py:227
  150.2 9.6 %all-to-all-done.1.refs_0_ = bf16[8,4,32,512]{3,2,1,0:T(8,128)(2,1)S(1)} async-done(((bf16[8,4,32,512]{3,2,1,0:T(8,128)(2,1)}), bf16[8,4,32,512]{3,2,1,0:T(8,128)(2,1)S(1)}, u32[]{:S(2)}, u32[]{:S(2)}) %all-to-all-start.1) | async-done | bytes 1048608 | tf_op jit(solution)/shard_map/all_to_all | solution.py:294
  159.7 1.0 copy-done.1
  160.7 14.6 %space_block.3 = bf16[2,4,256,1024]{3,2,1,0:T(8,128)(2,1)} custom-call(s32[2]{0:T(128)} %frame_count.7, s32[2]{0:T(128)} %token_count.3, bf16[2,4,256,1024]{3,2,1,0:T(8,128)(2,1)} %x_ref.7, bf16[8,4,32,512]{3,2,1,0:T(8,128)(2,1)} %copy-done.1, f32[1,1024]{1,0:T(1,128)} %bitcast.5, bf16[512,1024]{1,0:T(8,128)(2,1)} %refs_2_.3, ...), custom_call_target="tpu_custom_call", output_to_operand_aliasing={{}: (8, {})} | custom-call | flops 10737418240 | bytes 8000000 | tf_op jit(solution)/shard_map/space_block/pallas_call | solution.py:227
  (38 shorter events, 0.1 us)
Async XLA Ops:
  3.1 55.5 %all-to-all-start = ((bf16[8,4,32,1024]{3,2,1,0:T(8,128)(2,1)}), bf16[8,4,32,1024]{3,2,1,0:T(8,128)(2,1)S(1)}, u32[]{:S(2)}, u32[]{:S(2)}) async-start(bf16[8,4,32,1024]{3,2,1,0:T(8,128)(2,1)} %pack_tokens.3), calls=%async_computation | async-start | bytes 4194304 | tf_op jit(solution)/shard_map/all_to_all | solution.py:294
  58.6 16.3 %copy-start = (bf16[8,4,32,1024]{3,2,1,0:T(8,128)(2,1)}, bf16[8,4,32,1024]{3,2,1,0:T(8,128)(2,1)S(1)}, u32[]{:S(2)}) copy-start(bf16[8,4,32,1024]{3,2,1,0:T(8,128)(2,1)S(1)} %all-to-all-done.refs_0_) | copy-start | bytes 6291460
  58.6 7.3 %collective-permute-start = (bf16[4,32,1024]{2,1,0:T(8,128)(2,1)}, bf16[4,32,1024]{2,1,0:T(8,128)(2,1)S(1)}, u32[]{:S(2)}, u32[]{:S(2)}) collective-permute-start(bf16[4,32,1024]{2,1,0:T(8,128)(2,1)} %get-tuple-element.42), channel_id=1, source_target_pairs={{0,1},{1,0},{2,3},{3,2},{4,5},{5,4},{6,7},{7,6},{8,9},{9,8},{10,11... | collective-permute-start | bytes 786440 | tf_op jit(solution)/shard_map/ppermute | solution.py:298
  60.1 13.7 %collective-permute-start.3 = (bf16[4,32,1024]{2,1,0:T(8,128)(2,1)}, bf16[4,32,1024]{2,1,0:T(8,128)(2,1)S(1)}, u32[]{:S(2)}, u32[]{:S(2)}) collective-permute-start(bf16[4,32,1024]{2,1,0:T(8,128)(2,1)} %get-tuple-element.45), channel_id=1, source_target_pairs={{0,4},{1,5},{2,6},{3,7},{4,0},{5,1},{6,2},{7,3},{8,12},{9,13},{10,... | collective-permute-start | bytes 786440 | tf_op jit(solution)/shard_map/ppermute | solution.py:298
  60.1 26.5 %collective-permute-start.1 = (bf16[4,32,1024]{2,1,0:T(8,128)(2,1)}, bf16[4,32,1024]{2,1,0:T(8,128)(2,1)S(1)}, u32[]{:S(2)}, u32[]{:S(2)}) collective-permute-start(bf16[4,32,1024]{2,1,0:T(8,128)(2,1)} %get-tuple-element.43), channel_id=1, source_target_pairs={{0,2},{1,3},{2,0},{3,1},{4,6},{5,7},{6,4},{7,5},{8,10},{9,11},{10,... | collective-permute-start | bytes 786440 | tf_op jit(solution)/shard_map/ppermute | solution.py:298
  62.1 24.6 %collective-permute-start.2 = (bf16[4,32,1024]{2,1,0:T(8,128)(2,1)}, bf16[4,32,1024]{2,1,0:T(8,128)(2,1)S(1)}, u32[]{:S(2)}, u32[]{:S(2)}) collective-permute-start(bf16[4,32,1024]{2,1,0:T(8,128)(2,1)} %get-tuple-element.44), channel_id=1, source_target_pairs={{0,3},{1,2},{2,1},{3,0},{4,7},{5,6},{6,5},{7,4},{8,11},{9,10},{10,... | collective-permute-start | bytes 786440 | tf_op jit(solution)/shard_map/ppermute | solution.py:298
  62.9 23.8 %collective-permute-start.4 = (bf16[4,32,1024]{2,1,0:T(8,128)(2,1)}, bf16[4,32,1024]{2,1,0:T(8,128)(2,1)S(1)}, u32[]{:S(2)}, u32[]{:S(2)}) collective-permute-start(bf16[4,32,1024]{2,1,0:T(8,128)(2,1)} %get-tuple-element.46), channel_id=1, source_target_pairs={{0,5},{1,4},{2,7},{3,6},{4,1},{5,0},{6,3},{7,2},{8,13},{9,12},{10,... | collective-permute-start | bytes 786440 | tf_op jit(solution)/shard_map/ppermute | solution.py:298
  65.9 20.6 %copy-start.2 = (bf16[4,32,1024]{2,1,0:T(8,128)(2,1)}, bf16[4,32,1024]{2,1,0:T(8,128)(2,1)S(1)}, u32[]{:S(2)}) copy-start(bf16[4,32,1024]{2,1,0:T(8,128)(2,1)S(1)} %collective-permute-done.refs_1_) | copy-start | bytes 786436
  65.9 25.7 %collective-permute-start.5 = (bf16[4,32,1024]{2,1,0:T(8,128)(2,1)}, bf16[4,32,1024]{2,1,0:T(8,128)(2,1)S(1)}, u32[]{:S(2)}, u32[]{:S(2)}) collective-permute-start(bf16[4,32,1024]{2,1,0:T(8,128)(2,1)} %get-tuple-element.47), channel_id=1, source_target_pairs={{0,6},{1,7},{2,4},{3,5},{4,2},{5,3},{6,0},{7,1},{8,14},{9,15},{10,... | collective-permute-start | bytes 786440 | tf_op jit(solution)/shard_map/ppermute | solution.py:298
  73.8 12.8 %copy-start.3 = (bf16[4,32,1024]{2,1,0:T(8,128)(2,1)}, bf16[4,32,1024]{2,1,0:T(8,128)(2,1)S(1)}, u32[]{:S(2)}) copy-start(bf16[4,32,1024]{2,1,0:T(8,128)(2,1)S(1)} %collective-permute-done.3.refs_4_) | copy-start | bytes 786436
  73.8 24.9 %collective-permute-start.6 = (bf16[4,32,1024]{2,1,0:T(8,128)(2,1)}, bf16[4,32,1024]{2,1,0:T(8,128)(2,1)S(1)}, u32[]{:S(2)}, u32[]{:S(2)}) collective-permute-start(bf16[4,32,1024]{2,1,0:T(8,128)(2,1)} %get-tuple-element.48), channel_id=1, source_target_pairs={{0,7},{1,6},{2,5},{3,4},{4,3},{5,2},{6,1},{7,0},{8,15},{9,14},{10,... | collective-permute-start | bytes 786440 | tf_op jit(solution)/shard_map/ppermute | solution.py:298
  86.6 32.1 %copy-start.4 = (bf16[4,32,1024]{2,1,0:T(8,128)(2,1)}, bf16[4,32,1024]{2,1,0:T(8,128)(2,1)S(1)}, u32[]{:S(2)}) copy-start(bf16[4,32,1024]{2,1,0:T(8,128)(2,1)S(1)} %collective-permute-done.1.refs_2_) | copy-start | bytes 786436
  86.6 30.4 %collective-permute-start.7 = (bf16[4,32,512]{2,1,0:T(8,128)(2,1)}, bf16[4,32,512]{2,1,0:T(8,128)(2,1)S(1)}, u32[]{:S(2)}, u32[]{:S(2)}) collective-permute-start(bf16[4,32,512]{2,1,0:T(8,128)(2,1)} %get-tuple-element.50), channel_id=1, source_target_pairs={{0,4},{1,5},{2,6},{3,7},{4,0},{5,1},{6,2},{7,3},{8,12},{9,13},{10,... | collective-permute-start | bytes 393224 | tf_op jit(solution)/shard_map/ppermute | solution.py:298
  86.7 32.0 %copy-start.5 = (bf16[4,32,1024]{2,1,0:T(8,128)(2,1)}, bf16[4,32,1024]{2,1,0:T(8,128)(2,1)S(1)}, u32[]{:S(2)}) copy-start(bf16[4,32,1024]{2,1,0:T(8,128)(2,1)S(1)} %collective-permute-done.2.refs_3_) | copy-start | bytes 786436
  86.7 32.0 %copy-start.6 = (bf16[4,32,1024]{2,1,0:T(8,128)(2,1)}, bf16[4,32,1024]{2,1,0:T(8,128)(2,1)S(1)}, u32[]{:S(2)}) copy-start(bf16[4,32,1024]{2,1,0:T(8,128)(2,1)S(1)} %collective-permute-done.4.refs_5_) | copy-start | bytes 786436
  91.6 27.1 %copy-start.7 = (bf16[4,32,1024]{2,1,0:T(8,128)(2,1)}, bf16[4,32,1024]{2,1,0:T(8,128)(2,1)S(1)}, u32[]{:S(2)}) copy-start(bf16[4,32,1024]{2,1,0:T(8,128)(2,1)S(1)} %collective-permute-done.5.refs_6_) | copy-start | bytes 786436
  98.6 20.0 %copy-start.8 = (bf16[4,32,1024]{2,1,0:T(8,128)(2,1)}, bf16[4,32,1024]{2,1,0:T(8,128)(2,1)S(1)}, u32[]{:S(2)}) copy-start(bf16[4,32,1024]{2,1,0:T(8,128)(2,1)S(1)} %collective-permute-done.6.refs_7_) | copy-start | bytes 786436
  98.6 18.9 %collective-permute-start.12 = (bf16[4,32,512]{2,1,0:T(8,128)(2,1)}, bf16[4,32,512]{2,1,0:T(8,128)(2,1)S(1)}, u32[]{:S(2)}, u32[]{:S(2)}) collective-permute-start(bf16[4,32,512]{2,1,0:T(8,128)(2,1)} %get-tuple-element.60), channel_id=1, source_target_pairs={{0,3},{1,2},{2,1},{3,0},{4,7},{5,6},{6,5},{7,4},{8,11},{9,10},{10,... | collective-permute-start | bytes 393224 | tf_op jit(solution)/shard_map/ppermute | solution.py:298
  111.7 18.7 %collective-permute-start.11 = (bf16[4,32,512]{2,1,0:T(8,128)(2,1)}, bf16[4,32,512]{2,1,0:T(8,128)(2,1)S(1)}, u32[]{:S(2)}, u32[]{:S(2)}) collective-permute-start(bf16[4,32,512]{2,1,0:T(8,128)(2,1)} %get-tuple-element.58), channel_id=1, source_target_pairs={{0,6},{1,7},{2,4},{3,5},{4,2},{5,3},{6,0},{7,1},{8,14},{9,15},{10,... | collective-permute-start | bytes 393224 | tf_op jit(solution)/shard_map/ppermute | solution.py:298
  113.1 17.3 %collective-permute-start.10 = (bf16[4,32,512]{2,1,0:T(8,128)(2,1)}, bf16[4,32,512]{2,1,0:T(8,128)(2,1)S(1)}, u32[]{:S(2)}, u32[]{:S(2)}) collective-permute-start(bf16[4,32,512]{2,1,0:T(8,128)(2,1)} %get-tuple-element.56), channel_id=1, source_target_pairs={{0,2},{1,3},{2,0},{3,1},{4,6},{5,7},{6,4},{7,5},{8,10},{9,11},{10,... | collective-permute-start | bytes 393224 | tf_op jit(solution)/shard_map/ppermute | solution.py:298
  113.1 17.3 %collective-permute-start.9 = (bf16[4,32,512]{2,1,0:T(8,128)(2,1)}, bf16[4,32,512]{2,1,0:T(8,128)(2,1)S(1)}, u32[]{:S(2)}, u32[]{:S(2)}) collective-permute-start(bf16[4,32,512]{2,1,0:T(8,128)(2,1)} %get-tuple-element.54), channel_id=1, source_target_pairs={{0,5},{1,4},{2,7},{3,6},{4,1},{5,0},{6,3},{7,2},{8,13},{9,12},{10,... | collective-permute-start | bytes 393224 | tf_op jit(solution)/shard_map/ppermute | solution.py:298
  117.0 13.4 %copy-start.9 = (bf16[4,32,512]{2,1,0:T(8,128)(2,1)}, bf16[4,32,512]{2,1,0:T(8,128)(2,1)S(1)}, u32[]{:S(2)}) copy-start(bf16[4,32,512]{2,1,0:T(8,128)(2,1)S(1)} %collective-permute-done.7.refs_4_) | copy-start | bytes 393220
  117.0 13.5 %collective-permute-start.8 = (bf16[4,32,512]{2,1,0:T(8,128)(2,1)}, bf16[4,32,512]{2,1,0:T(8,128)(2,1)S(1)}, u32[]{:S(2)}, u32[]{:S(2)}) collective-permute-start(bf16[4,32,512]{2,1,0:T(8,128)(2,1)} %get-tuple-element.52), channel_id=1, source_target_pairs={{0,1},{1,0},{2,3},{3,2},{4,5},{5,4},{6,7},{7,6},{8,9},{9,8},{10,11... | collective-permute-start | bytes 393224 | tf_op jit(solution)/shard_map/ppermute | solution.py:298
  117.5 12.8 %copy-start.10 = (bf16[4,32,512]{2,1,0:T(8,128)(2,1)}, bf16[4,32,512]{2,1,0:T(8,128)(2,1)S(1)}, u32[]{:S(2)}) copy-start(bf16[4,32,512]{2,1,0:T(8,128)(2,1)S(1)} %collective-permute-done.12.refs_3_) | copy-start | bytes 393220
  117.5 12.9 %collective-permute-start.13 = (bf16[4,32,512]{2,1,0:T(8,128)(2,1)}, bf16[4,32,512]{2,1,0:T(8,128)(2,1)S(1)}, u32[]{:S(2)}, u32[]{:S(2)}) collective-permute-start(bf16[4,32,512]{2,1,0:T(8,128)(2,1)} %get-tuple-element.62), channel_id=1, source_target_pairs={{0,7},{1,6},{2,5},{3,4},{4,3},{5,2},{6,1},{7,0},{8,15},{9,14},{10,... | collective-permute-start | bytes 393224 | tf_op jit(solution)/shard_map/ppermute | solution.py:298
  130.4 5.0 %copy-start.11 = (bf16[4,32,512]{2,1,0:T(8,128)(2,1)}, bf16[4,32,512]{2,1,0:T(8,128)(2,1)S(1)}, u32[]{:S(2)}) copy-start(bf16[4,32,512]{2,1,0:T(8,128)(2,1)S(1)} %collective-permute-done.11.refs_6_) | copy-start | bytes 393220
  130.4 5.0 %copy-start.12 = (bf16[4,32,512]{2,1,0:T(8,128)(2,1)}, bf16[4,32,512]{2,1,0:T(8,128)(2,1)S(1)}, u32[]{:S(2)}) copy-start(bf16[4,32,512]{2,1,0:T(8,128)(2,1)S(1)} %collective-permute-done.10.refs_2_) | copy-start | bytes 393220
  130.4 5.0 %copy-start.13 = (bf16[4,32,512]{2,1,0:T(8,128)(2,1)}, bf16[4,32,512]{2,1,0:T(8,128)(2,1)S(1)}, u32[]{:S(2)}) copy-start(bf16[4,32,512]{2,1,0:T(8,128)(2,1)S(1)} %collective-permute-done.9.refs_5_) | copy-start | bytes 393220
  130.4 5.0 %copy-start.14 = (bf16[4,32,512]{2,1,0:T(8,128)(2,1)}, bf16[4,32,512]{2,1,0:T(8,128)(2,1)S(1)}, u32[]{:S(2)}) copy-start(bf16[4,32,512]{2,1,0:T(8,128)(2,1)S(1)} %collective-permute-done.8.refs_1_) | copy-start | bytes 393220
  130.4 4.9 %copy-start.15 = (bf16[4,32,512]{2,1,0:T(8,128)(2,1)}, bf16[4,32,512]{2,1,0:T(8,128)(2,1)S(1)}, u32[]{:S(2)}) copy-start(bf16[4,32,512]{2,1,0:T(8,128)(2,1)S(1)} %collective-permute-done.13.refs_7_) | copy-start | bytes 393220
  130.4 29.3 %all-to-all-start.1 = ((bf16[8,4,32,512]{3,2,1,0:T(8,128)(2,1)}), bf16[8,4,32,512]{3,2,1,0:T(8,128)(2,1)S(1)}, u32[]{:S(2)}, u32[]{:S(2)}) async-start(bf16[8,4,32,512]{3,2,1,0:T(8,128)(2,1)} %time_attention.2), calls=%async_computation.1 | async-start | bytes 2097152 | tf_op jit(solution)/shard_map/all_to_all | solution.py:294
  159.7 1.0 copy-start.1
